TPU v7x, 128 devices: a whole 4x4x4 slice. The times are simulated.
128 devices in a mesh: row: 16 (over z, x), col: 8 (over y, core).
Axes of the slice: x: 4, y: 4, z: 4, core: 2. Of those that a mesh axis runs over, the one named last changes fastest.
Arguments:
- fine_coeffs: float32 [2048, 4096], P(('row', 'col')), may hold values from -6 to 6
- fine_slot: int32 [2048], P(('row', 'col')), may hold values from 0 to 2047, as said below
- neighbours: int32 [256, 6], P('row'), may hold values from -1 to 255, as said below
- filter_matrix: float32 [32, 32], replicated, may hold values from -1 to 1
- kernel_ops: float32 [20, 3, 3, 1024], replicated, may hold values from -0.625 to 0.625
Outputs:
- fine_result: float32 [2048, 4096], P(('row', 'col'))
Inputs may be any that keep to these rules, and one draw needn't show every extreme that they name: `fine_slot`: every value appears once. Run r holds the parents r * 16 to (r + 1) * 16 - 1. A fine box on a device with col index c has its parent in the c-th block of 2 consecutive parents of the parent's run. Of the 16 fine boxes of one device, at most 2 have parents in one run, and some device has exactly 2 in some run. -1 where the grid of parents ends. neighbours[neighbours[p, d], d XOR 1] = p. For a parent of run r, the neighbours in directions 0, 2, 4 lie in run (r + 1) mod 16 and those in directions 1, 3, 5 in run (r - 1) mod 16.
All inputs are finite; a program needn't handle non-finite values.
Results may differ from a plain program's by a relative error of at most 0.0001.
Values sent between devices are 32-bit elements; how exact they have to be, the bound alone decides.
A program may use at most 64 MiB of HBM per device.

v0:
```python
import functools

import jax
import jax.numpy as jnp
from jax import lax
from jax.experimental import pallas as pl
from jax.experimental.pallas import tpu as pltpu
from jax.sharding import PartitionSpec as P

exact_mode = lax.Precision.HIGHEST
f32, bf16 = jnp.float32, jnp.bfloat16
TERMS, N, PAIRS = 20, 32, 10


def split(x):
    hi = x.astype(bf16)
    return hi, (x - hi.astype(f32)).astype(bf16)


def dot(a, b):
    return jnp.dot(a, b, preferred_element_type=f32)


def dot_t(a, b):
    return lax.dot_general(a, b, (((1,), (1,)), ((), ())), preferred_element_type=f32)


def packed_rows(x):
    hi, lo = split(x)
    return jnp.concatenate([hi, lo, hi], axis=1)


def low_half(rows):
    return lax.broadcasted_iota(jnp.int32, (rows, 128), 1) < 64


def centre_pass(xk, wz, wy, wx, t_hi, t_lo, ys, out):
    mask = low_half(N)

    def pair(mp, carry):
        weights = wz[pl.ds(pl.multiple_of(mp * 128, 128), 128), 0:192]
        for q in range(4):
            z = dot_t(xk[q * 256 : (q + 1) * 256, :], weights)
            hi, lo = split(z)
            t_hi[q * 256 : (q + 1) * 256, 0:128] = hi
            t_lo[q * 256 : (q + 1) * 256, 0:128] = lo
        left = jnp.concatenate([wy[mp * 2, 0:N, 0:96], wy[mp * 2 + 1, 0:N, 0:96]], axis=0)

        def line(i8, carry):
            for k in range(8):
                i = i8 * 8 + k
                at = pl.ds(pl.multiple_of(i * N, N), N)
                hi, lo = t_hi[at, 0:128], t_lo[at, 0:128]
                y = dot(left, jnp.concatenate([hi, lo, hi], axis=0))
                ys[pl.ds(mp * N + i, N, stride=PAIRS * N), :] = jnp.where(mask, y[:N], y[N:])
            return carry

        return lax.fori_loop(0, N // 8, line, carry)

    lax.fori_loop(0, PAIRS, pair, 0)

    def column(b, carry):
        at = pl.ds(pl.multiple_of(b * PAIRS * N, PAIRS * N), PAIRS * N)
        hi, lo = split(ys[at, :])
        first = dot(wx[:, 0:320], hi)
        r = first[:64] + first[64:] + dot(wx[0:64, 0:320], lo)
        out[pl.ds(pl.multiple_of(b * N, N), N), :] = r[:N] + pltpu.roll(r[N:], 64, 1)
        return carry

    lax.fori_loop(0, N, column, 0, unroll=2)


def sides_pass(xkb, xka, wzb, wza, wy, wx, wx0, t_hi, t_lo, ya, yb, yc, out):
    mask = low_half(N)

    def pair(mp, carry):
        for xk, wz, base in ((xkb, wzb, 0), (xka, wza, 128)):
            weights = wz[pl.ds(pl.multiple_of(mp * 256, 256), 256), 0:192]
            for q in range(4):
                z = dot_t(xk[q * 256 : (q + 1) * 256, :], weights)
                hi, lo = split(z)
                for odd in range(2):
                    t_hi[odd * 1024 + q * 256 : odd * 1024 + (q + 1) * 256, base : base + 128] = hi[
                        :, odd * 128 : (odd + 1) * 128
                    ]
                    t_lo[odd * 1024 + q * 256 : odd * 1024 + (q + 1) * 256, base : base + 128] = lo[
                        :, odd * 128 : (odd + 1) * 128
                    ]
        for odd in range(2):
            m = mp * 2 + odd
            left = wy[m, :, 0:96]

            def line(i8, carry, odd=odd, m=m, left=left):
                for k in range(8):
                    i = i8 * 8 + k
                    at = pl.ds(pl.multiple_of(odd * 1024 + i * N, N), N)
                    hi, lo = t_hi[at, :], t_lo[at, :]
                    y = dot(left, jnp.concatenate([hi, lo, hi], axis=0))
                    to = pl.ds(m * N + i, N, stride=TERMS * N)
                    ya[to, :] = y[:N, :128]
                    yb[to, :] = y[:N, 128:]
                    yc[to, :] = jnp.where(mask, y[N : 2 * N, :128], y[2 * N :, 128:])
                return carry

            lax.fori_loop(0, N // 8, line, 0)
        return carry

    lax.fori_loop(0, PAIRS, pair, 0)

    def column(b, carry):
        at = pl.ds(pl.multiple_of(b * TERMS * N, TERMS * N), TERMS * N)
        rows = pl.ds(pl.multiple_of(b * N, N), N)
        hi, lo = split(ya[at, :])
        first = dot(wx[0:128, :], hi)
        r = first[:64] + first[64:128] + dot(wx[0:64, :], lo)
        out[rows, 0:128] = jnp.where(mask, r[:N], r[N:])
        hi, lo = split(yb[at, :])
        first = dot(wx[128:256, :], hi)
        r = first[:64] + first[64:128] + dot(wx[128:192, :], lo)
        out[rows, 128:256] = jnp.where(mask, r[:N], r[N:])
        hi, lo = split(yc[at, :])
        first = dot(wx0[...], hi)
        out[rows, 256:384] = first[:N] + first[N:] + dot(wx0[0:N, :], lo)
        return carry

    lax.fori_loop(0, N, column, 0)


def kernel(xo, xb, xa, wzo, wzb, wza, wys, wxo, wxs, wx0, sel, part, centre,
           xk, xkb, t_hi, t_lo, yo, ya, yb, yc, terms):
    xk[...] = packed_rows(xo[...])
    centre_pass(xk, wzo, wys, wxo, t_hi, t_lo, yo, centre)
    xk[...] = packed_rows(xa[...])
    xkb[...] = packed_rows(xb[...])
    sides_pass(xkb, xk, wzb, wza, wys, wxs, wx0, t_hi, t_lo, ya, yb, yc, terms)
    for q in range(4):
        rows = slice(q * 256, (q + 1) * 256)
        hi, lo = split(terms[rows, :])
        summed = dot(hi, sel[...]) + dot(lo, sel[...])
        for y in range(4):
            part[y, rows, :] = summed[:, y * 128 : (y + 1) * 128]


def convolve(xo, xb, xa, weights, sel):
    vm = pl.BlockSpec(memory_space=pltpu.VMEM)
    operands = (xo, xb, xa, *weights, sel)
    return pl.pallas_call(
        kernel,
        out_shape=(
            jax.ShapeDtypeStruct((4, 1024, 128), f32),
            jax.ShapeDtypeStruct((1024, 128), f32),
        ),
        in_specs=[vm] * len(operands),
        out_specs=(vm, vm),
        scratch_shapes=[
            pltpu.VMEM((1024, 192), bf16),
            pltpu.VMEM((1024, 192), bf16),
            pltpu.VMEM((2048, 256), bf16),
            pltpu.VMEM((2048, 256), bf16),
            pltpu.VMEM((N * PAIRS * N, 128), f32),
            pltpu.VMEM((N * TERMS * N, 128), f32),
            pltpu.VMEM((N * TERMS * N, 128), f32),
            pltpu.VMEM((N * TERMS * N, 128), f32),
            pltpu.VMEM((1024, 384), f32),
        ],
        compiler_params=pltpu.CompilerParams(vmem_limit_bytes=60 * 2**20),
    )(*operands)


def take(array, axis, places):
    return jnp.stack([lax.index_in_dim(array, k, axis, False) for k in places], axis)


def fold_kernel(f, hx, ht, wzo, wzb, wza, wys, wxo, wxs, wx0, k_hi, k_lo, folded, mats):
    def row(a, carry):
        hi, lo = split(hx[pl.ds(a, 1), :] * ht[...])
        at = pl.ds(pl.multiple_of(a * N, N), N)
        k_hi[at, :] = hi
        k_lo[at, :] = lo
        return carry

    lax.fori_loop(0, N, row, 0)
    f_hi, f_lo = split(f[...])
    for n in range(4):
        at = slice(n * 256, (n + 1) * 256)
        folded[:, at] = dot(f_hi, k_hi[:, at]) + dot(f_lo, k_hi[:, at]) + dot(f_hi, k_lo[:, at])
    for g in range(8):
        piece = folded[:, g * 128 : (g + 1) * 128]
        for k in range(4):
            turned = piece if k == 0 else pltpu.roll(piece, 128 - 32 * k, 1)
            mats[pl.ds(4 * g + k, 192, stride=N), :] = turned
    mask = lax.broadcasted_iota(jnp.int32, (N, 128), 1) < N

    def matrix(m, axis, offset):
        start = (m * 9 + axis * 3 + offset) * N
        v = mats[pl.ds(start if isinstance(m, int) else pl.multiple_of(start, N), N), :]
        return jnp.where(mask, v, 0.0)

    def parts(v):
        hi = v.astype(bf16).astype(f32)
        return hi, v - hi

    def term(m, carry):
        for t, offset in enumerate((1, 2, 0)):
            hi, lo = parts(matrix(m, 1, offset))
            wys[m, t * N : (t + 1) * N, :] = (hi + pltpu.roll(hi, 32, 1) + pltpu.roll(lo, 64, 1)).astype(bf16)
        for offset, places in ((0, ((wza, 0),)), (1, ((wzo, 0), (wzb, 0), (wza, 64))), (2, ((wzb, 64),))):
            hi, lo = parts(matrix(m, 2, offset))
            first = hi + pltpu.roll(hi, 64, 1)
            for ref, base in places:
                start = m * (64 if ref is wzo else 128) + base
                for p in range(2):
                    at = pl.ds(pl.multiple_of(start + p * N, N), N)
                    ref[at, 0:128] = (pltpu.roll(first, 32, 1) if p else first).astype(bf16)
                    ref[at, 128:256] = (pltpu.roll(lo, 32, 1) if p else lo).astype(bf16)
        return carry

    lax.fori_loop(0, TERMS, term, 0)

    def wide(terms, offset):
        total = None
        for k, m in enumerate(terms):
            v = matrix(m, 0, offset)
            v = pltpu.roll(v, 32 * k, 1) if k else v
            total = v if total is None else total + v
        return split(total)

    for g in range(5):
        at = slice(g * 128, (g + 1) * 128)
        for offset, places in ((2, ((wxs, 0, 64),)), (1, ((wxs, 32, 96), (wxs, 128, 192), (wx0, 0, 32))), (0, ((wxs, 160, 224),))):
            hi, lo = wide(range(4 * g, 4 * g + 4), offset)
            for ref, high_at, low_at in places:
                ref[high_at : high_at + N, at] = hi
                ref[low_at : low_at + N, at] = lo
    for g in range(3):
        at = slice(g * 128, (g + 1) * 128)
        for odd in range(2):
            hi, lo = wide([2 * mp + odd for mp in range(4 * g, min(4 * g + 4, PAIRS))], 1)
            wxo[odd * N : (odd + 1) * N, at] = hi
            wxo[64 + odd * N : 64 + (odd + 1) * N, at] = lo


def prepare(filter_matrix, kernel_ops):
    f = jnp.pad(kernel_ops.reshape(TERMS * 9, N * N), ((0, 12), (0, 0)))
    hx = jnp.repeat(filter_matrix, N, axis=1)
    ht = jnp.tile(filter_matrix, (1, N))
    vm = pl.BlockSpec(memory_space=pltpu.VMEM)
    shapes = ((1280, 256), (2560, 256), (2560, 256), (TERMS, 96, 128), (128, 384), (256, 640), (64, 640))
    return pl.pallas_call(
        fold_kernel,
        out_shape=tuple(jax.ShapeDtypeStruct(shape, bf16) for shape in shapes),
        in_specs=[vm] * 3,
        out_specs=(vm,) * len(shapes),
        scratch_shapes=[
            pltpu.VMEM((1024, 1024), bf16),
            pltpu.VMEM((1024, 1024), bf16),
            pltpu.VMEM((192, 1024), f32),
            pltpu.VMEM((192 * N, 128), f32),
        ],
        compiler_params=pltpu.CompilerParams(vmem_limit_bytes=40 * 2**20),
    )(f, hx, ht)


MESH = pl.DeviceIdType.MESH
Y, CORES, ROWS = 4, 2, 16


def return_kernel(part, centre, held, slot, out, from_core, pair_sum, from_y, total, from_half,
                  applied, boxes, leaving, back, s1, r1, s2, r2, s3, r3, s4, r4):
    row, col = lax.axis_index("row"), lax.axis_index("col")
    y, core = col // CORES, col % CORES
    sibling = y * CORES + (1 - core)
    peers = [(row, sibling)]
    peers += [(row, (y + 1 + d) % Y * CORES + core) for d in range(Y - 1)]
    peers += [((row + d) % ROWS, col) for d in range(1, ROWS)]
    barrier = pltpu.get_barrier_semaphore()
    for peer in peers:
        pl.semaphore_signal(barrier, inc=1, device_id=peer, device_id_type=MESH)
    pl.semaphore_wait(barrier, len(peers))
    mine = pl.ds(pl.multiple_of(core * 512, 512), 512)
    other = pl.ds(pl.multiple_of((1 - core) * 512, 512), 512)

    def send(src, dst, s, r, peer):
        copy = pltpu.make_async_remote_copy(
            src_ref=src, dst_ref=dst, send_sem=s, recv_sem=r, device_id=peer, device_id_type=MESH
        )
        copy.start()
        return copy

    order = [(y + 1 + d) % Y for d in range(Y)]
    first = [
        send(part.at[to, other], from_core.at[d], s1.at[d], r1.at[d], (row, sibling))
        for d, to in enumerate(order)
    ]
    second = []
    for d, to in enumerate(order):
        first[d].wait_recv()
        if d < Y - 1:
            pair_sum[d] = part[to, mine, :] + from_core[d]
            second.append(
                send(pair_sum.at[d], from_y.at[d], s2.at[d], r2.at[d], (row, to * CORES + core))
            )
        else:
            total[...] = part[to, mine, :] + from_core[d]
    for copy in second:
        copy.wait_recv()
    total[...] = total[...] + from_y[0] + from_y[1] + from_y[2]
    third = send(total, from_half, s3, r3, (row, sibling))

    def own_lanes(v):
        return jnp.where(core == 1, pltpu.roll(v, 64, 1), v)

    applied[mine, :] = own_lanes(total[...]) + centre[mine, :]
    third.wait_recv()
    applied[other, :] = own_lanes(from_half[...]) + centre[other, :]
    lanes = lax.broadcasted_iota(jnp.int32, (16, 128), 1) // 16
    for ox in range(2):
        for oy in range(2):
            for jh in range(2):
                lines = [
                    applied[pl.ds((oy * 16 + jh * 8 + j) * N + ox * 16, 16), :] for j in range(8)
                ]
                for p in range(2):
                    for oz in range(2):
                        base = p * 32 + oz * 16
                        box = None
                        for j in range(8):
                            shift = (16 * j - base) % 128
                            v = pltpu.roll(lines[j], shift, 1) if shift else lines[j]
                            box = v if box is None else jnp.where(lanes == j, v, box)
                        boxes[p * 8 + ox * 4 + oy * 2 + oz, pl.ds(jh, 16, stride=2), :] = box
    fourth = []
    for d in range(1, ROWS):
        to = (row + d) % ROWS
        for s in range(2):
            leaving[d * 2 + s] = boxes[held[to * 2 + s]]
        fourth.append(
            send(
                leaving.at[pl.ds(d * 2, 2)],
                back.at[pl.ds(row * 2, 2)],
                s4.at[d],
                r4.at[d],
                (to, col),
            )
        )
    for s in range(2):
        back[row * 2 + s] = boxes[held[row * 2 + s]]
    for copy in fourth:
        copy.wait_recv()
    for q in range(16):
        out[q] = back[slot[q]]
    for copy in first + second + [third] + fourth:
        copy.wait_send()


def gather_back(part, centre, held, slot):
    vm = pl.BlockSpec(memory_space=pltpu.VMEM)
    sm = pl.BlockSpec(memory_space=pltpu.SMEM)
    sems = [pltpu.SemaphoreType.DMA((n,)) for n in (4, 4, 3, 3)]
    sems += [pltpu.SemaphoreType.DMA, pltpu.SemaphoreType.DMA]
    sems += [pltpu.SemaphoreType.DMA((ROWS,)), pltpu.SemaphoreType.DMA((ROWS,))]
    return pl.pallas_call(
        return_kernel,
        out_shape=jax.ShapeDtypeStruct((16, 32, 128), f32),
        in_specs=[vm, vm, sm, sm],
        out_specs=vm,
        scratch_shapes=[
            pltpu.VMEM((4, 512, 128), f32),
            pltpu.VMEM((3, 512, 128), f32),
            pltpu.VMEM((3, 512, 128), f32),
            pltpu.VMEM((512, 128), f32),
            pltpu.VMEM((512, 128), f32),
            pltpu.VMEM((1024, 128), f32),
            pltpu.VMEM((16, 32, 128), f32),
            pltpu.VMEM((32, 32, 128), f32),
            pltpu.VMEM((32, 32, 128), f32),
        ]
        + sems,
        compiler_params=pltpu.CompilerParams(
            collective_id=2, has_side_effects=True, vmem_limit_bytes=32 * 2**20
        ),
    )(part, centre, held, slot)


def selection(neighbours, col_index):
    order = (1, 5, 4, 0, 3, 2)
    sender = take(neighbours, 1, order)
    within = sender % 16 - col_index * 2
    hit = (sender >= 0)[:, :, None] & (within[:, :, None] == jnp.arange(2)[None, None, :])
    hit = jnp.transpose(hit, (1, 2, 0)).astype(bf16)
    return (
        hit[:, :, None, :, None] * jnp.eye(N, dtype=bf16)[None, None, :, None, :]
    ).reshape(384, 512)


def shifted(array, axis, by):
    peers = lax.axis_size(axis)
    return lax.ppermute(array, axis, [(i, (i + by) % peers) for i in range(peers)])


def local(fine_coeffs, fine_slot, neighbours, filter_matrix, kernel_ops):
    row_count = lax.axis_size("row")
    held_boxes, volume = fine_coeffs.shape
    par_row = neighbours.shape[0]
    source_count = held_boxes // 8
    capacity = 2
    col_index = lax.axis_index("col")
    weights = prepare(filter_matrix, kernel_ops)
    dest_row = fine_slot // (8 * par_row)
    item = jnp.arange(held_boxes)
    earlier = (dest_row[None, :] == dest_row[:, None]) & (item[None, :] < item[:, None])
    slot_index = dest_row * capacity + jnp.sum(earlier.astype(jnp.int32), axis=1)
    packer = jnp.arange(row_count * capacity)[:, None] == slot_index[None, :]
    send_blocks = jnp.dot(packer.astype(f32), fine_coeffs, precision=exact_mode)
    send_ids = jnp.max(jnp.where(packer, fine_slot[None, :], -1), axis=1)
    a2a = functools.partial(
        lax.all_to_all, axis_name="row", split_axis=0, concat_axis=0, tiled=True
    )
    got_blocks = a2a(send_blocks.reshape(row_count, capacity, volume))
    got_ids = a2a(send_ids.reshape(row_count, capacity)).reshape(-1)
    child_pos = got_ids % held_boxes
    picker = (
        (child_pos[None, :] == jnp.arange(held_boxes)[:, None]) & (got_ids[None, :] >= 0)
    ).astype(f32)
    children = jnp.dot(picker, got_blocks.reshape(-1, volume), precision=exact_mode)
    boxes = children.reshape(source_count, 2, 2, 2, 16, 16, 16)
    own = jnp.transpose(boxes, (1, 4, 2, 5, 0, 3, 6)).reshape(1024, 64)
    below, above = shifted(own, "row", 1), shifted(own, "row", -1)
    part, centre = convolve(own, below, above, weights, selection(neighbours, col_index))
    held = jnp.where(got_ids >= 0, child_pos, 0)
    return gather_back(part, centre, held, slot_index).reshape(held_boxes, volume)


def solution(mesh):
    in_specs = (P(("row", "col"), None), P(("row", "col")), P("row", None), P(), P())
    out_specs = P(("row", "col"), None)
    return jax.shard_map(local, mesh=mesh, in_specs=in_specs, out_specs=out_specs, check_vma=False)
```

profile of v0, /device:TPU:0, one launch (start us, length us, event | category | flops | bytes accessed | tf_op | source)
XLA Modules:
  0.0 180.1 jit_solution(3897447404558869801)
XLA Ops:
  0.0 0.0 copy-start
  0.0 0.7 and_select_fusion.1
  0.7 0.2 convert_reduce_fusion
  0.9 0.7 multiply_add_fusion.1.slot
  1.6 0.7 select_reduce_fusion
  2.3 0.7 all_to_all.9
  3.0 8.0 %all-to-all-start = ((s32[16,1,2]{2,1,0:T(1,128)}), s32[16,1,2]{2,1,0:T(1,128)S(1)}, u32[]{:S(2)}, u32[]{:S(2)}) async-start(s32[16,1,2]{2,1,0:T(1,128)} %bitcast), calls=%async_computation | async-start | bytes 16384 | tf_op jit(solution)/shard_map/all_to_all | solution.py:420
  11.0 0.9 fusion.14
  11.9 0.0 copy-done
  11.9 0.5 fusion.4
  12.5 1.1 reshape.289
  13.6 4.9 %all-to-all-done = s32[16,1,2]{2,1,0:T(1,128)S(1)} async-done(((s32[16,1,2]{2,1,0:T(1,128)}), s32[16,1,2]{2,1,0:T(1,128)S(1)}, u32[]{:S(2)}, u32[]{:S(2)}) %all-to-all-start) | async-done | bytes 160 | tf_op jit(solution)/shard_map/all_to_all | solution.py:420
  18.4 3.6 %all-to-all-start.1 = ((f32[16,2,4096]{2,1,0:T(2,128)}), f32[16,2,4096]{2,1,0:T(2,128)S(1)}, u32[]{:S(2)}, u32[]{:S(2)}) async-start(f32[16,2,4096]{2,1,0:T(2,128)} %reshape.289), calls=%async_computation.1 | async-start | bytes 1048576 | tf_op jit(solution)/shard_map/all_to_all | solution.py:419
  22.1 0.2 tile.10.ht
  22.3 0.2 broadcast_in_dim.17
  22.5 0.2 reshape.293.hx
  22.8 1.7 copy.27
  24.5 0.4 reshape.292
  24.8 0.5 broadcast.147
  25.3 0.7 reduce.3
  26.0 0.1 reshape.288
  26.1 6.3 %all-to-all-done.1 = f32[16,2,4096]{2,1,0:T(2,128)S(1)} async-done(((f32[16,2,4096]{2,1,0:T(2,128)}), f32[16,2,4096]{2,1,0:T(2,128)S(1)}, u32[]{:S(2)}, u32[]{:S(2)}) %all-to-all-start.1) | async-done | bytes 524320 | tf_op jit(solution)/shard_map/all_to_all | solution.py:419
  32.4 1.2 reshape.290
  33.6 1.6 copy.23
  35.2 7.5 %convolution_bitcast_fusion = f32[2,16,2,16,2,2,16]{6,5,3,1,2,0,4:T(2,128)S(1)} fusion(f32[16,16,16,32,1,1,1]{3,2,1,0,6,5,4:T(8,128)S(1)} %bitcast.28, pred[32]{0:T(512)(128)(4,1)S(1)} %broadcast_compare_fusion, s32[2,2,2,2]{3,2,1,0:T(2,128)S(1)} %multiply_add_fusion, s32[32]{0:T(128)S(1)} %get-tuple-element.24), kind=kOutput, calls=%fused_computation | convolution fusion | flops 25166848 | bytes 786656 | tf_op jit(solution)/shard_map/dot_general | solution.py:425
  42.8 0.7 copy.31
  43.5 2.4 %reshape.297.xo = f32[1024,64]{1,0:T(8,128)} reshape(f32[2,16,2,16,2,2,16]{6,5,4,3,2,1,0:T(2,128)S(1)} %copy.31) | data formatting | bytes 524288 | tf_op jit(solution)/shard_map/reshape | solution.py:427
  45.9 1.2 collective-permute-start.1
  47.1 0.9 collective-permute-start
  47.9 0.2 broadcast_multiply_fusion
  48.1 2.3 %mul.28.sel = bf16[384,512]{1,0:T(8,128)(2,1)} reshape(bf16[6,2,32,16,32]{4,3,2,1,0:T(8,128)(2,1)S(1)} %broadcast_multiply_fusion) | data formatting | bytes 786432 | tf_op jit(solution)/shard_map/mul | solution.py:392
  50.4 0.1 pad.4.f
  50.5 7.8 %shard_map.55 = (bf16[1280,256]{1,0:T(8,128)(2,1)S(1)}, bf16[2560,256]{1,0:T(8,128)(2,1)S(1)}, bf16[2560,256]{1,0:T(8,128)(2,1)S(1)}, bf16[20,96,128]{2,1,0:T(8,...) custom-call(f32[192,1024]{1,0:T(8,128)S(1)} %pad.4.f, ...), custom_call_target="tpu_custom_call" | custom-call | tf_op jit(solution)/shard_map/pallas_call | solution.py:249
  58.3 1.1 copy-done.2
  59.4 1.1 copy-done.3
  60.5 0.8 copy-done.4
  61.3 0.8 copy-done.6
  62.1 0.7 copy-done.7
  62.8 0.6 copy-done.8
  63.5 0.6 copy-done.9
  64.1 0.0 collective-permute-done.1.xa
  64.1 0.0 collective-permute-done.xb
  64.1 0.8 copy-done.10
  64.9 80.6 %shard_map.56 = (f32[4,1024,128]{2,1,0:T(8,128)}, f32[1024,128]{1,0:T(8,128)}) custom-call(f32[1024,64]{1,0:T(8,128)} %reshape.297.xo, f32[1024,64]{1,0:T(8,128)} %collective-permute-done.xb, f32[1024,64]{1,0:T(8,128)} %copy-done.10, bf16[1280,256]{1,0:T(8,128)(2,1)} %copy-done.4, bf16[2560,256]{1,0:T(8,128)(2,1)} %copy-done.2, bf16[2560,256]{1,0:T(8,128)(2,1)} %copy-done.3, ...), custom_call_target="tpu_custom_call" | custom-call | tf_op jit(solution)/shard_map/pallas_call | solution.py:147
  145.5 1.6 copy-done.1
  147.1 1.0 copy-done.5
  148.2 31.0 %shard_map.57 = f32[16,32,128]{2,1,0:T(8,128)S(1)} custom-call(f32[4,1024,128]{2,1,0:T(8,128)S(1)} %copy-done.1, f32[1024,128]{1,0:T(8,128)S(1)} %copy-done.5, s32[32]{0:T(128)S(1)} %get-tuple-element.23.held, s32[16]{0:T(128)S(1)} %multiply_add_fusion.1.slot), custom_call_target="tpu_custom_call" | custom-call | tf_op jit(solution)/shard_map/pallas_call | solution.py:362
  179.2 0.9 copy.35
  (21 shorter events, 0.1 us)
Async XLA Ops:
  0.0 11.9 %copy-start = (f32[16,4096]{1,0:T(8,128)S(1)}, f32[16,4096]{1,0:T(8,128)}, u32[]{:S(2)}) copy-start(f32[16,4096]{1,0:T(8,128)} %param.5) | copy-start | bytes 786436
  0.0 22.0 %copy-start.11 = (f32[32,32]{1,0:T(8,128)S(1)}, f32[32,32]{1,0:T(8,128)}, u32[]{:S(2)}) copy-start(f32[32,32]{1,0:T(8,128)} %param.8) | copy-start | bytes 12292
  3.0 15.4 %all-to-all-start = ((s32[16,1,2]{2,1,0:T(1,128)}), s32[16,1,2]{2,1,0:T(1,128)S(1)}, u32[]{:S(2)}, u32[]{:S(2)}) async-start(s32[16,1,2]{2,1,0:T(1,128)} %bitcast), calls=%async_computation | async-start | bytes 16384 | tf_op jit(solution)/shard_map/all_to_all | solution.py:420
  18.4 14.0 %all-to-all-start.1 = ((f32[16,2,4096]{2,1,0:T(2,128)}), f32[16,2,4096]{2,1,0:T(2,128)S(1)}, u32[]{:S(2)}, u32[]{:S(2)}) async-start(f32[16,2,4096]{2,1,0:T(2,128)} %reshape.289), calls=%async_computation.1 | async-start | bytes 1048576 | tf_op jit(solution)/shard_map/all_to_all | solution.py:419
  45.9 18.2 %collective-permute-start.1 = (f32[1024,64]{1,0:T(8,128)}, f32[1024,64]{1,0:T(8,128)S(1)}, u32[]{:S(2)}, u32[]{:S(2)}) collective-permute-start(f32[1024,64]{1,0:T(8,128)} %reshape.297.xo), channel_id=1, source_target_pairs={{0,120},{8,0},{16,8},{24,16},{32,24},{40,32},{48,40},{56,48},{64,5... | collective-permute-start | bytes 786440 | tf_op jit(solution)/shard_map/ppermute | solution.py:398
  47.1 17.0 %collective-permute-start = (f32[1024,64]{1,0:T(8,128)}, f32[1024,64]{1,0:T(8,128)}, u32[]{:S(2)}, u32[]{:S(2)}) collective-permute-start(f32[1024,64]{1,0:T(8,128)} %reshape.297.xo), channel_id=1, source_target_pairs={{0,8},{8,16},{16,24},{24,32},{32,40},{40,48},{48,56},{56,64},{64,7... | collective-permute-start | bytes 786440 | tf_op jit(solution)/shard_map/ppermute | solution.py:398
  58.3 1.1 copy-start.2
  59.4 1.1 copy-start.3
  60.5 0.8 copy-start.4
  61.3 0.8 copy-start.6
  62.1 0.7 copy-start.7
  62.8 0.6 copy-start.8
  63.5 0.6 copy-start.9
  64.1 0.8 copy-start.10
  145.5 1.6 copy-start.1
  147.1 1.0 copy-start.5
where the time goes:
time: 181 us; the launch traced here: 180 us
  Pallas kernels  119 us (66%)
  local copies, waits for them, and re-layouts  24.4 us (13%)
  starting transfers between devices  13.6 us (8%)
  waiting for transfers between devices  11.2 us (6%)
  matrix products  8.01 us (4%)
  other arithmetic  3.2 us (2%)
    pallas_call x1, Pallas kernels, convolve(): pl.pallas_call(kernel, out_shape=(jax.ShapeDtypeStruct((4, 1024, 128), f3...  80.6 us
    pallas_call x1, Pallas kernels, gather_back(): pl.pallas_call(return_kernel, out_shape=jax.ShapeDtypeStruct((16, 32, 128...  31 us
    unnamed x26, local copies, waits for them, and re-layouts  11.7 us
    all_to_all x1, starting transfers between devices, local(): got_ids = a2a(send_ids.reshape(row_count, capacity)).reshape(-1)  7.96 us
    pallas_call x1, Pallas kernels, prepare(): pl.pallas_call(fold_kernel, out_shape=tuple((jax.ShapeDtypeStruct(shape,...  7.83 us
    dot_general x1, matrix products, local(): jnp.dot(picker, got_blocks.reshape(-1, volume), precision=exact_mode)  7.53 us
    all_to_all x1, waiting for transfers between devices, local(): got_blocks = a2a(send_blocks.reshape(row_count, capacity, volume))  6.28 us
    all_to_all x1, waiting for transfers between devices, local(): got_ids = a2a(send_ids.reshape(row_count, capacity)).reshape(-1)  4.88 us
  transfers between devices with their start and end apart: 4, of which 2 were waited for; matrix products, arithmetic and copies ran while one was open for 5% of the time, Pallas kernels for 4%

commit v1 on v0

--- a/solution.py
+++ b/solution.py
@@ -1,5 +1,3 @@
-import functools
-
 import jax
 import jax.numpy as jnp
 from jax import lax
@@ -7,9 +5,9 @@
 from jax.experimental.pallas import tpu as pltpu
 from jax.sharding import PartitionSpec as P
 
-exact_mode = lax.Precision.HIGHEST
 f32, bf16 = jnp.float32, jnp.bfloat16
 TERMS, N, PAIRS = 20, 32, 10
+SIDE_LINE, OWN_LINE = TERMS * N + 8, PAIRS * N + 8
 
 
 def split(x):
@@ -25,11 +23,6 @@
     return lax.dot_general(a, b, (((1,), (1,)), ((), ())), preferred_element_type=f32)
 
 
-def packed_rows(x):
-    hi, lo = split(x)
-    return jnp.concatenate([hi, lo, hi], axis=1)
-
-
 def low_half(rows):
     return lax.broadcasted_iota(jnp.int32, (rows, 128), 1) < 64
 
@@ -40,34 +33,30 @@
     def pair(mp, carry):
         weights = wz[pl.ds(pl.multiple_of(mp * 128, 128), 128), 0:192]
         for q in range(4):
-            z = dot_t(xk[q * 256 : (q + 1) * 256, :], weights)
+            z = dot_t(xk[q * 256 : (q + 1) * 256, 0:192], weights)
             hi, lo = split(z)
             t_hi[q * 256 : (q + 1) * 256, 0:128] = hi
             t_lo[q * 256 : (q + 1) * 256, 0:128] = lo
         left = jnp.concatenate([wy[mp * 2, 0:N, 0:96], wy[mp * 2 + 1, 0:N, 0:96]], axis=0)
 
-        def line(i8, carry):
-            for k in range(8):
-                i = i8 * 8 + k
-                at = pl.ds(pl.multiple_of(i * N, N), N)
-                hi, lo = t_hi[at, 0:128], t_lo[at, 0:128]
-                y = dot(left, jnp.concatenate([hi, lo, hi], axis=0))
-                ys[pl.ds(mp * N + i, N, stride=PAIRS * N), :] = jnp.where(mask, y[:N], y[N:])
-            return carry
-
-        return lax.fori_loop(0, N // 8, line, carry)
+        for i in range(N):
+            at = slice(i * N, (i + 1) * N)
+            hi, lo = t_hi[at, 0:128], t_lo[at, 0:128]
+            y = dot(left, jnp.concatenate([hi, lo, hi], axis=0))
+            ys[pl.ds(mp * N + i, N, stride=OWN_LINE), :] = jnp.where(mask, y[:N], y[N:])
+        return carry
 
     lax.fori_loop(0, PAIRS, pair, 0)
 
     def column(b, carry):
-        at = pl.ds(pl.multiple_of(b * PAIRS * N, PAIRS * N), PAIRS * N)
+        at = pl.ds(pl.multiple_of(b * OWN_LINE, 8), PAIRS * N)
         hi, lo = split(ys[at, :])
         first = dot(wx[:, 0:320], hi)
         r = first[:64] + first[64:] + dot(wx[0:64, 0:320], lo)
         out[pl.ds(pl.multiple_of(b * N, N), N), :] = r[:N] + pltpu.roll(r[N:], 64, 1)
         return carry
 
-    lax.fori_loop(0, N, column, 0, unroll=2)
+    lax.fori_loop(0, N, column, 0, unroll=4)
 
 
 def sides_pass(xkb, xka, wzb, wza, wy, wx, wx0, t_hi, t_lo, ya, yb, yc, out):
@@ -77,7 +66,7 @@
         for xk, wz, base in ((xkb, wzb, 0), (xka, wza, 128)):
             weights = wz[pl.ds(pl.multiple_of(mp * 256, 256), 256), 0:192]
             for q in range(4):
-                z = dot_t(xk[q * 256 : (q + 1) * 256, :], weights)
+                z = dot_t(xk[q * 256 : (q + 1) * 256, 0:192], weights)
                 hi, lo = split(z)
                 for odd in range(2):
                     t_hi[odd * 1024 + q * 256 : odd * 1024 + (q + 1) * 256, base : base + 128] = hi[
@@ -90,25 +79,20 @@
             m = mp * 2 + odd
             left = wy[m, :, 0:96]
 
-            def line(i8, carry, odd=odd, m=m, left=left):
-                for k in range(8):
-                    i = i8 * 8 + k
-                    at = pl.ds(pl.multiple_of(odd * 1024 + i * N, N), N)
-                    hi, lo = t_hi[at, :], t_lo[at, :]
-                    y = dot(left, jnp.concatenate([hi, lo, hi], axis=0))
-                    to = pl.ds(m * N + i, N, stride=TERMS * N)
-                    ya[to, :] = y[:N, :128]
-                    yb[to, :] = y[:N, 128:]
-                    yc[to, :] = jnp.where(mask, y[N : 2 * N, :128], y[2 * N :, 128:])
-                return carry
-
-            lax.fori_loop(0, N // 8, line, 0)
+            for i in range(N):
+                at = slice(odd * 1024 + i * N, odd * 1024 + (i + 1) * N)
+                hi, lo = t_hi[at, :], t_lo[at, :]
+                y = dot(left, jnp.concatenate([hi, lo, hi], axis=0))
+                to = pl.ds(m * N + i, N, stride=SIDE_LINE)
+                ya[to, :] = y[:N, :128]
+                yb[to, :] = y[:N, 128:]
+                yc[to, :] = jnp.where(mask, y[N : 2 * N, :128], y[2 * N :, 128:])
         return carry
 
     lax.fori_loop(0, PAIRS, pair, 0)
 
     def column(b, carry):
-        at = pl.ds(pl.multiple_of(b * TERMS * N, TERMS * N), TERMS * N)
+        at = pl.ds(pl.multiple_of(b * SIDE_LINE, 8), TERMS * N)
         rows = pl.ds(pl.multiple_of(b * N, N), N)
         hi, lo = split(ya[at, :])
         first = dot(wx[0:128, :], hi)
@@ -123,16 +107,13 @@
         out[rows, 256:384] = first[:N] + first[N:] + dot(wx0[0:N, :], lo)
         return carry
 
-    lax.fori_loop(0, N, column, 0)
-
-
-def kernel(xo, xb, xa, wzo, wzb, wza, wys, wxo, wxs, wx0, sel, part, centre,
-           xk, xkb, t_hi, t_lo, yo, ya, yb, yc, terms):
-    xk[...] = packed_rows(xo[...])
-    centre_pass(xk, wzo, wys, wxo, t_hi, t_lo, yo, centre)
-    xk[...] = packed_rows(xa[...])
-    xkb[...] = packed_rows(xb[...])
-    sides_pass(xkb, xk, wzb, wza, wys, wxs, wx0, t_hi, t_lo, ya, yb, yc, terms)
+    lax.fori_loop(0, N, column, 0, unroll=4)
+
+
+def kernel(xs, wzo, wzb, wza, wys, wxo, wxs, wx0, sel, part, centre,
+           t_hi, t_lo, yo, ya, yb, yc, terms):
+    centre_pass(xs.at[0], wzo, wys, wxo, t_hi, t_lo, yo, centre)
+    sides_pass(xs.at[1], xs.at[2], wzb, wza, wys, wxs, wx0, t_hi, t_lo, ya, yb, yc, terms)
     for q in range(4):
         rows = slice(q * 256, (q + 1) * 256)
         hi, lo = split(terms[rows, :])
@@ -141,9 +122,9 @@
             part[y, rows, :] = summed[:, y * 128 : (y + 1) * 128]
 
 
-def convolve(xo, xb, xa, weights, sel):
+def convolve(xs, weights, sel):
     vm = pl.BlockSpec(memory_space=pltpu.VMEM)
-    operands = (xo, xb, xa, *weights, sel)
+    operands = (xs, *weights, sel)
     return pl.pallas_call(
         kernel,
         out_shape=(
@@ -153,14 +134,12 @@
         in_specs=[vm] * len(operands),
         out_specs=(vm, vm),
         scratch_shapes=[
-            pltpu.VMEM((1024, 192), bf16),
-            pltpu.VMEM((1024, 192), bf16),
             pltpu.VMEM((2048, 256), bf16),
             pltpu.VMEM((2048, 256), bf16),
-            pltpu.VMEM((N * PAIRS * N, 128), f32),
-            pltpu.VMEM((N * TERMS * N, 128), f32),
-            pltpu.VMEM((N * TERMS * N, 128), f32),
-            pltpu.VMEM((N * TERMS * N, 128), f32),
+            pltpu.VMEM((N * OWN_LINE, 128), f32),
+            pltpu.VMEM((N * SIDE_LINE, 128), f32),
+            pltpu.VMEM((N * SIDE_LINE, 128), f32),
+            pltpu.VMEM((N * SIDE_LINE, 128), f32),
             pltpu.VMEM((1024, 384), f32),
         ],
         compiler_params=pltpu.CompilerParams(vmem_limit_bytes=60 * 2**20),
@@ -171,7 +150,7 @@
     return jnp.stack([lax.index_in_dim(array, k, axis, False) for k in places], axis)
 
 
-def fold_kernel(f, hx, ht, wzo, wzb, wza, wys, wxo, wxs, wx0, k_hi, k_lo, folded, mats):
+def fold(f, hx, ht, wzo, wzb, wza, wys, wxo, wxs, wx0, k_hi, k_lo, folded, mats):
     def row(a, carry):
         hi, lo = split(hx[pl.ds(a, 1), :] * ht[...])
         at = pl.ds(pl.multiple_of(a * N, N), N)
@@ -240,29 +219,135 @@
             wxo[64 + odd * N : 64 + (odd + 1) * N, at] = lo
 
 
-def prepare(filter_matrix, kernel_ops):
+MESH = pl.DeviceIdType.MESH
+Y, CORES, ROWS = 4, 2, 16
+
+
+def start_copy(src, dst, s, r, peer):
+    copy = pltpu.make_async_remote_copy(
+        src_ref=src, dst_ref=dst, send_sem=s, recv_sem=r, device_id=peer, device_id_type=MESH
+    )
+    copy.start()
+    return copy
+
+
+def greet(peers):
+    barrier = pltpu.get_barrier_semaphore()
+    for peer in peers:
+        pl.semaphore_signal(barrier, inc=1, device_id=peer, device_id_type=MESH)
+    pl.semaphore_wait(barrier, len(peers))
+
+
+BOX_LINE = N + 8
+
+
+def lay_out(boxes, lines, xs):
+    piece = lax.broadcasted_iota(jnp.int32, (16, 128), 1) // 16
+
+    def octant(at, carry):
+        ox, oy, jh = at // 4, at // 2 % 2, at % 2
+        rows = [boxes[p * 8 + ox * 4 + oy * 2 + oz, pl.ds(jh, 16, stride=2), :] for p in range(2) for oz in range(2)]
+        for j in range(8):
+            x = None
+            for k in range(4):
+                shift = (16 * (k - j)) % 128
+                v = pltpu.roll(rows[k], shift, 1) if shift else rows[k]
+                x = v if x is None else jnp.where(piece == k, v, x)
+            lines[pl.ds(ox * 16 * BOX_LINE + oy * 16 + jh * 8 + j, 16, stride=BOX_LINE), :] = x
+        return carry
+
+    lax.fori_loop(0, 8, octant, 0)
+    mask = low_half(N)
+
+    def line(i, carry):
+        v = lines[pl.ds(pl.multiple_of(i * BOX_LINE, 8), N), :]
+        hi = v.astype(bf16).astype(f32)
+        at = pl.ds(pl.multiple_of(i * N, N), N)
+        xs[at, 0:128] = jnp.where(mask, hi, pltpu.roll(v - hi, 64, 1)).astype(bf16)
+        xs[at, 128:256] = v.astype(bf16)
+        return carry
+
+    lax.fori_loop(0, N, line, 0, unroll=4)
+
+
+def exchange_kernel(fine, tags, source, f, hx, ht, xs, came_from, wzo, wzb, wza, wys, wxo, wxs, wx0,
+                    k_hi, k_lo, folded, mats, leaving, arrived, boxes, lines, s1, r1, s2, r2):
+    row, col = lax.axis_index("row"), lax.axis_index("col")
+    greet([((row + d) % ROWS, col) for d in range(1, ROWS)])
+    copies = []
+    for d in list(range(1, ROWS)) + [0]:
+        to = (row + d) % ROWS
+        target = arrived.at[row] if d == 0 else leaving.at[d]
+        target[0:32, :] = fine[source[2 * to]]
+        target[32:64, :] = fine[source[2 * to + 1]]
+        target[64:72, :] = tags[to]
+        if d:
+            copies.append(start_copy(leaving.at[d], arrived.at[row], s1.at[d], r1.at[d], (to, col)))
+    fold(f, hx, ht, wzo, wzb, wza, wys, wxo, wxs, wx0, k_hi, k_lo, folded, mats)
+    for copy in copies:
+        copy.wait_recv()
+
+    def place(at, carry):
+        wanted = at.astype(f32)
+        total = [jnp.zeros((8, 128), f32)] * 4
+        for k in range(ROWS):
+            for s in range(2):
+                hit = jnp.broadcast_to(arrived[k, 64 + s : 65 + s, :], (8, 128)) == wanted
+                for c in range(4):
+                    start = s * 32 + c * 8
+                    total[c] = jnp.where(hit, arrived[k, start : start + 8, :], total[c])
+        for c in range(4):
+            boxes[0, at, c * 8 : (c + 1) * 8, :] = total[c]
+        return carry
+
+    lax.fori_loop(0, 16, place, 0)
+    up, down = (row + 1) % ROWS, (row + ROWS - 1) % ROWS
+    hops = [
+        start_copy(boxes.at[0], boxes.at[1], s2.at[0], r2.at[0], (up, col)),
+        start_copy(boxes.at[0], boxes.at[2], s2.at[1], r2.at[1], (down, col)),
+    ]
+    for k in range(ROWS):
+        came_from[k] = arrived[k, 64:72, :]
+    lay_out(boxes.at[0], lines, xs.at[0])
+    for hop, k in zip(hops, (1, 2)):
+        hop.wait_recv()
+        lay_out(boxes.at[k], lines, xs.at[k])
+    for copy in copies + hops:
+        copy.wait_send()
+
+
+def exchange(fine, tags, source, filter_matrix, kernel_ops):
     f = jnp.pad(kernel_ops.reshape(TERMS * 9, N * N), ((0, 12), (0, 0)))
     hx = jnp.repeat(filter_matrix, N, axis=1)
     ht = jnp.tile(filter_matrix, (1, N))
     vm = pl.BlockSpec(memory_space=pltpu.VMEM)
+    sm = pl.BlockSpec(memory_space=pltpu.SMEM)
     shapes = ((1280, 256), (2560, 256), (2560, 256), (TERMS, 96, 128), (128, 384), (256, 640), (64, 640))
+    shapes = tuple(jax.ShapeDtypeStruct(shape, bf16) for shape in shapes)
+    outs = (jax.ShapeDtypeStruct((3, 1024, 256), bf16), jax.ShapeDtypeStruct((16, 8, 128), f32)) + shapes
     return pl.pallas_call(
-        fold_kernel,
-        out_shape=tuple(jax.ShapeDtypeStruct(shape, bf16) for shape in shapes),
-        in_specs=[vm] * 3,
-        out_specs=(vm,) * len(shapes),
+        exchange_kernel,
+        out_shape=outs,
+        in_specs=[vm, vm, sm, vm, vm, vm],
+        out_specs=(vm,) * len(outs),
         scratch_shapes=[
             pltpu.VMEM((1024, 1024), bf16),
             pltpu.VMEM((1024, 1024), bf16),
             pltpu.VMEM((192, 1024), f32),
             pltpu.VMEM((192 * N, 128), f32),
+            pltpu.VMEM((16, 72, 128), f32),
+            pltpu.VMEM((16, 72, 128), f32),
+            pltpu.VMEM((3, 16, 32, 128), f32),
+            pltpu.VMEM((N * BOX_LINE, 128), f32),
+            pltpu.SemaphoreType.DMA((ROWS,)),
+            pltpu.SemaphoreType.DMA((ROWS,)),
+            pltpu.SemaphoreType.DMA((2,)),
+            pltpu.SemaphoreType.DMA((2,)),
         ],
-        compiler_params=pltpu.CompilerParams(vmem_limit_bytes=40 * 2**20),
-    )(f, hx, ht)
-
-
-MESH = pl.DeviceIdType.MESH
-Y, CORES, ROWS = 4, 2, 16
+        compiler_params=pltpu.CompilerParams(
+            collective_id=1, has_side_effects=True, vmem_limit_bytes=40 * 2**20
+        ),
+    )(fine, tags, source, f, hx, ht)
 
 
 def return_kernel(part, centre, held, slot, out, from_core, pair_sum, from_y, total, from_half,
@@ -273,23 +358,13 @@
     peers = [(row, sibling)]
     peers += [(row, (y + 1 + d) % Y * CORES + core) for d in range(Y - 1)]
     peers += [((row + d) % ROWS, col) for d in range(1, ROWS)]
-    barrier = pltpu.get_barrier_semaphore()
-    for peer in peers:
-        pl.semaphore_signal(barrier, inc=1, device_id=peer, device_id_type=MESH)
-    pl.semaphore_wait(barrier, len(peers))
+    greet(peers)
     mine = pl.ds(pl.multiple_of(core * 512, 512), 512)
     other = pl.ds(pl.multiple_of((1 - core) * 512, 512), 512)
 
-    def send(src, dst, s, r, peer):
-        copy = pltpu.make_async_remote_copy(
-            src_ref=src, dst_ref=dst, send_sem=s, recv_sem=r, device_id=peer, device_id_type=MESH
-        )
-        copy.start()
-        return copy
-
     order = [(y + 1 + d) % Y for d in range(Y)]
     first = [
-        send(part.at[to, other], from_core.at[d], s1.at[d], r1.at[d], (row, sibling))
+        start_copy(part.at[to, other], from_core.at[d], s1.at[d], r1.at[d], (row, sibling))
         for d, to in enumerate(order)
     ]
     second = []
@@ -298,14 +373,14 @@
         if d < Y - 1:
             pair_sum[d] = part[to, mine, :] + from_core[d]
             second.append(
-                send(pair_sum.at[d], from_y.at[d], s2.at[d], r2.at[d], (row, to * CORES + core))
+                start_copy(pair_sum.at[d], from_y.at[d], s2.at[d], r2.at[d], (row, to * CORES + core))
             )
         else:
             total[...] = part[to, mine, :] + from_core[d]
     for copy in second:
         copy.wait_recv()
     total[...] = total[...] + from_y[0] + from_y[1] + from_y[2]
-    third = send(total, from_half, s3, r3, (row, sibling))
+    third = start_copy(total, from_half, s3, r3, (row, sibling))
 
     def own_lanes(v):
         return jnp.where(core == 1, pltpu.roll(v, 64, 1), v)
@@ -335,7 +410,7 @@
         for s in range(2):
             leaving[d * 2 + s] = boxes[held[to * 2 + s]]
         fourth.append(
-            send(
+            start_copy(
                 leaving.at[pl.ds(d * 2, 2)],
                 back.at[pl.ds(row * 2, 2)],
                 s4.at[d],
@@ -393,41 +468,21 @@
     ).reshape(384, 512)
 
 
-def shifted(array, axis, by):
-    peers = lax.axis_size(axis)
-    return lax.ppermute(array, axis, [(i, (i + by) % peers) for i in range(peers)])
-
-
 def local(fine_coeffs, fine_slot, neighbours, filter_matrix, kernel_ops):
-    row_count = lax.axis_size("row")
     held_boxes, volume = fine_coeffs.shape
-    par_row = neighbours.shape[0]
-    source_count = held_boxes // 8
-    capacity = 2
-    col_index = lax.axis_index("col")
-    weights = prepare(filter_matrix, kernel_ops)
-    dest_row = fine_slot // (8 * par_row)
+    dest_row = fine_slot // 128
     item = jnp.arange(held_boxes)
     earlier = (dest_row[None, :] == dest_row[:, None]) & (item[None, :] < item[:, None])
-    slot_index = dest_row * capacity + jnp.sum(earlier.astype(jnp.int32), axis=1)
-    packer = jnp.arange(row_count * capacity)[:, None] == slot_index[None, :]
-    send_blocks = jnp.dot(packer.astype(f32), fine_coeffs, precision=exact_mode)
-    send_ids = jnp.max(jnp.where(packer, fine_slot[None, :], -1), axis=1)
-    a2a = functools.partial(
-        lax.all_to_all, axis_name="row", split_axis=0, concat_axis=0, tiled=True
-    )
-    got_blocks = a2a(send_blocks.reshape(row_count, capacity, volume))
-    got_ids = a2a(send_ids.reshape(row_count, capacity)).reshape(-1)
-    child_pos = got_ids % held_boxes
-    picker = (
-        (child_pos[None, :] == jnp.arange(held_boxes)[:, None]) & (got_ids[None, :] >= 0)
-    ).astype(f32)
-    children = jnp.dot(picker, got_blocks.reshape(-1, volume), precision=exact_mode)
-    boxes = children.reshape(source_count, 2, 2, 2, 16, 16, 16)
-    own = jnp.transpose(boxes, (1, 4, 2, 5, 0, 3, 6)).reshape(1024, 64)
-    below, above = shifted(own, "row", 1), shifted(own, "row", -1)
-    part, centre = convolve(own, below, above, weights, selection(neighbours, col_index))
-    held = jnp.where(got_ids >= 0, child_pos, 0)
+    slot_index = dest_row * 2 + jnp.sum(earlier.astype(jnp.int32), axis=1)
+    packer = jnp.arange(2 * ROWS)[:, None] == slot_index[None, :]
+    source = jnp.sum(jnp.where(packer, item[None, :], 0), axis=1)
+    places = jnp.max(jnp.where(packer, fine_slot[None, :] % 16, -1), axis=1).astype(f32)
+    tags = jnp.broadcast_to(places.reshape(ROWS, 2, 1), (ROWS, 2, 128))
+    tags = jnp.pad(tags, ((0, 0), (0, 6), (0, 0)))
+    boxes = fine_coeffs.reshape(held_boxes, 32, 128)
+    xs, came_from, *weights = exchange(boxes, tags, source, filter_matrix, kernel_ops)
+    part, centre = convolve(xs, weights, selection(neighbours, lax.axis_index("col")))
+    held = jnp.maximum(came_from[:, 0:2, 0].reshape(2 * ROWS).astype(jnp.int32), 0)
     return gather_back(part, centre, held, slot_index).reshape(held_boxes, volume)
 
 

time: 181 us -> 114 us (0.63)
  Pallas kernels: 119 us -> 94.8 us
  starting transfers between devices: 13.6 us -> 0 us
  waiting for transfers between devices: 11.2 us -> 0 us
  matrix products: 8.01 us -> 0 us
  local copies, waits for them, and re-layouts: 24.4 us -> 17.3 us
    pallas_call x1, Pallas kernels: 80.6 us -> 36.2 us  [convolve(): pl.pallas_call(kernel, out_shape=(jax.ShapeDtypeStruct((4, 1024, 128), f3...]
    pallas_call x1, Pallas kernels: 7.83 us -> 29.6 us  [exchange(): pl.pallas_call(exchange_kernel, out_shape=outs, in_specs=[vm, vm, sm, vm,...]
    all_to_all x2 -> x0, starting transfers between devices: 11.5 us -> none  [the longest x1 7.96 us: local(): got_ids = a2a(send_ids.reshape(row_count, capacity)).reshape(-1)]
    all_to_all x2 -> x0, waiting for transfers between devices: 11.2 us -> none  [the longest x1 6.28 us: local(): got_blocks = a2a(send_blocks.reshape(row_count, capacity, volume))]
    dot_general x2 -> x0, matrix products: 8.01 us -> none  [the longest x1 7.53 us: local(): jnp.dot(picker, got_blocks.reshape(-1, volume), precision=exact_mode)]
    reshape x8 -> x2, local copies, waits for them, and re-layouts: 7.74 us -> 0.61 us  [the longest x1 0.37 us: exchange(): f = jnp.pad(kernel_ops.reshape(TERMS * 9, N * N), ((0, 12), (0, 0)))]
    ppermute x2 -> x0, starting transfers between devices: 2.03 us -> none  [shifted(): lax.ppermute(array, axis, [(i, (i + by) % peers) for i in range(peers)])]
    pallas_call x1, Pallas kernels: 31 us -> 29 us  [gather_back(): pl.pallas_call(return_kernel, out_shape=jax.ShapeDtypeStruct((16, 32, 128...]
  transfers between devices with their start and end apart: 4 -> 0, of which waited for: 2 -> 0; matrix products, arithmetic and copies ran while one was open for 5% -> 0% of each run, Pallas kernels for 4% -> 0%
where the time goes in v1:
time: 114 us
  Pallas kernels  94.8 us (83%)
  local copies, waits for them, and re-layouts  17.3 us (15%)
  other arithmetic  1.6 us (1%)
    pallas_call x1, Pallas kernels, convolve(): pl.pallas_call(kernel, out_shape=(jax.ShapeDtypeStruct((4, 1024, 128), f3...  36.2 us
    pallas_call x1, Pallas kernels, exchange(): pl.pallas_call(exchange_kernel, out_shape=outs, in_specs=[vm, vm, sm, vm,...  29.6 us
    pallas_call x1, Pallas kernels, gather_back(): pl.pallas_call(return_kernel, out_shape=jax.ShapeDtypeStruct((16, 32, 128...  29 us
    unnamed x27, local copies, waits for them, and re-layouts  12 us
    mul x1, local copies, waits for them, and re-layouts, selection(): hit[:, :, None, :, None] * jnp.eye(N, dtype=bf16)[None, None, :, None, :]  2.3 us

profile of v1, /device:TPU:0, one launch (start us, length us, event | category | flops | bytes accessed | tf_op | source)
XLA Modules:
  0.0 113.8 jit_solution(96178923555318964)
XLA Ops:
  0.0 0.0 copy-start.11
  0.0 0.0 copy-start.10
  0.0 0.7 and_select_fusion
  0.7 0.2 convert_reduce_fusion
  0.9 0.1 select_reduce_fusion
  1.0 0.9 fusion.5
  2.0 0.1 convert_element_type.37
  2.1 0.1 broadcast_in_dim.43
  2.2 1.0 copy.9
  3.2 0.8 tile.4
  4.0 0.2 tile.10.ht
  4.2 0.0 copy-done.11
  4.2 0.2 broadcast_in_dim.46
  4.4 0.2 reshape.228.hx
  4.7 0.0 copy-done.10
  4.7 0.5 copy.8
  5.2 0.4 reshape.227
  5.6 0.1 pad.9.f
  5.7 0.2 broadcast_multiply_fusion
  5.8 2.3 %mul.28.sel = bf16[384,512]{1,0:T(8,128)(2,1)} reshape(bf16[6,2,32,16,32]{4,3,2,1,0:T(8,128)(2,1)S(1)} %broadcast_multiply_fusion) | data formatting | bytes 786432 | tf_op jit(solution)/shard_map/mul | solution.py:467
  8.1 29.6 %shard_map.55 = (bf16[3,1024,256]{2,1,0:T(8,128)(2,1)S(1)}, f32[16,8,128]{2,1,0:T(8,128)S(1)}, bf16[1280,256]{1,0:T(8,128)(2,1)S(1)}, bf16[2560,256]{1,0:T(8,128...) custom-call(f32[16,32,128]{2,1,0:T(8,128)S(1)} %bitcast.12, ...), custom_call_target="tpu_custom_call" | custom-call | tf_op jit(solution)/shard_map/pallas_call | solution.py:328
  37.7 0.0 copy-start.1
  37.7 1.1 %copy-done.1 = bf16[3,1024,256]{2,1,0:T(8,128)(2,1)} copy-done((bf16[3,1024,256]{2,1,0:T(8,128)(2,1)}, bf16[3,1024,256]{2,1,0:T(8,128)(2,1)S(1)}, u32[]{:S(2)}) %copy-start.1) | copy-done | bytes 1572888
  38.9 0.0 copy-start.2
  38.9 1.1 copy-done.2
  40.0 0.0 copy-start.3
  40.0 1.1 copy-done.3
  41.0 0.0 copy-start.4
  41.0 0.8 copy-done.4
  41.9 0.0 copy-start.6
  41.9 0.8 copy-done.6
  42.7 0.0 copy-start.7
  42.7 0.8 copy-done.7
  43.4 0.0 copy-start.8
  43.4 0.6 copy-done.8
  44.1 0.0 copy-start.9
  44.1 0.6 copy-done.9
  44.7 36.2 %shard_map.56 = (f32[4,1024,128]{2,1,0:T(8,128)}, f32[1024,128]{1,0:T(8,128)}) custom-call(bf16[3,1024,256]{2,1,0:T(8,128)(2,1)} %copy-done.1, bf16[1280,256]{1,0:T(8,128)(2,1)} %copy-done.4, bf16[2560,256]{1,0:T(8,128)(2,1)} %copy-done.2, bf16[2560,256]{1,0:T(8,128)(2,1)} %copy-done.3, bf16[20,96,128]{2,1,0:T(8,128)(2,1)} %copy-done.6, ...), custom_call_target="tpu_custom_call" | custom-call | tf_op jit(solution)/shard_map/pallas_call | solution.py:128
  80.9 0.3 maximum_reduce_fusion
  81.2 0.1 max.10.held
  81.3 0.0 copy-start
  81.3 1.6 %copy-done = f32[4,1024,128]{2,1,0:T(8,128)S(1)} copy-done((f32[4,1024,128]{2,1,0:T(8,128)S(1)}, f32[4,1024,128]{2,1,0:T(8,128)}, u32[]{:S(2)}) %copy-start) | copy-done | bytes 2097176
  82.9 0.0 copy-start.5
  82.9 1.0 copy-done.5
  83.9 29.0 %shard_map.57 = f32[16,32,128]{2,1,0:T(8,128)S(1)} custom-call(f32[4,1024,128]{2,1,0:T(8,128)S(1)} %copy-done, f32[1024,128]{1,0:T(8,128)S(1)} %copy-done.5, s32[32]{0:T(128)S(1)} %max.10.held, s32[16]{0:T(128)S(1)} %multiply_add_fusion.slot), custom_call_target="tpu_custom_call" | custom-call | tf_op jit(solution)/shard_map/pallas_call | solution.py:437
  113.0 0.9 copy.12
  (8 shorter events, 0.1 us)
Async XLA Ops:
  0.0 4.2 %copy-start.11 = (f32[32,32]{1,0:T(8,128)S(1)}, f32[32,32]{1,0:T(8,128)}, u32[]{:S(2)}) copy-start(f32[32,32]{1,0:T(8,128)} %param.8) | copy-start | bytes 12292
  0.0 4.7 %copy-start.10 = (f32[20,3,3,1024]{3,0,2,1:T(8,128)S(1)}, f32[20,3,3,1024]{3,0,2,1:T(8,128)}, u32[]{:S(2)}) copy-start(f32[20,3,3,1024]{3,0,2,1:T(8,128)} %param.9) | copy-start | bytes 2211844
  37.7 1.2 %copy-start.1 = (bf16[3,1024,256]{2,1,0:T(8,128)(2,1)}, bf16[3,1024,256]{2,1,0:T(8,128)(2,1)S(1)}, u32[]{:S(2)}) copy-start(bf16[3,1024,256]{2,1,0:T(8,128)(2,1)S(1)} %get-tuple-element.16.xs) | copy-start | bytes 4718596
  38.9 1.1 copy-start.2
  40.0 1.1 copy-start.3
  41.0 0.8 copy-start.4
  41.9 0.8 copy-start.6
  42.7 0.8 copy-start.7
  43.4 0.6 copy-start.8
  44.1 0.6 copy-start.9
  81.3 1.6 %copy-start = (f32[4,1024,128]{2,1,0:T(8,128)S(1)}, f32[4,1024,128]{2,1,0:T(8,128)}, u32[]{:S(2)}) copy-start(f32[4,1024,128]{2,1,0:T(8,128)} %get-tuple-element.24.part) | copy-start | bytes 6291460
  82.9 1.0 copy-start.5

commit v2 on v1

v2 whole, which is shorter than its diff:
```python
import jax
import jax.numpy as jnp
from jax import lax
from jax.experimental import pallas as pl
from jax.experimental.pallas import tpu as pltpu
from jax.sharding import PartitionSpec as P

f32, bf16 = jnp.float32, jnp.bfloat16
TERMS, N, PAIRS = 20, 32, 10
SIDE_LINE, OWN_LINE, MAT_LINE = TERMS * N + 8, PAIRS * N + 8, N + 8


def split(x):
    hi = x.astype(bf16)
    return hi, (x - hi.astype(f32)).astype(bf16)


def dot(a, b):
    return jnp.dot(a, b, preferred_element_type=f32)


def dot_t(a, b):
    return lax.dot_general(a, b, (((1,), (1,)), ((), ())), preferred_element_type=f32)


def low_half(rows):
    return lax.broadcasted_iota(jnp.int32, (rows, 128), 1) < 64


def centre_pass(xk, wz, wy, wx, t_hi, t_lo, ys, out):
    mask = low_half(N)

    def pair(mp, carry):
        weights = wz[pl.ds(pl.multiple_of(mp * 128, 128), 128), 0:192]
        for q in range(4):
            z = dot_t(xk[q * 256 : (q + 1) * 256, 0:192], weights)
            hi, lo = split(z)
            t_hi[q * 256 : (q + 1) * 256, 0:128] = hi
            t_lo[q * 256 : (q + 1) * 256, 0:128] = lo
        left = jnp.concatenate([wy[mp * 2, 0:N, 0:96], wy[mp * 2 + 1, 0:N, 0:96]], axis=0)

        for i in range(N):
            at = slice(i * N, (i + 1) * N)
            hi, lo = t_hi[at, 0:128], t_lo[at, 0:128]
            y = dot(left, jnp.concatenate([hi, lo, hi], axis=0))
            ys[pl.ds(mp * N + i, N, stride=OWN_LINE), :] = jnp.where(mask, y[:N], y[N:])
        return carry

    lax.fori_loop(0, PAIRS, pair, 0)

    def column(b, carry):
        at = pl.ds(pl.multiple_of(b * OWN_LINE, 8), PAIRS * N)
        hi, lo = split(ys[at, :])
        first = dot(wx[:, 0:320], hi)
        r = first[:64] + first[64:] + dot(wx[0:64, 0:320], lo)
        out[pl.ds(pl.multiple_of(b * N, N), N), :] = r[:N] + pltpu.roll(r[N:], 64, 1)
        return carry

    lax.fori_loop(0, N, column, 0, unroll=4)


def sides_lines(xkb, xka, wzb, wza, wy, t_hi, t_lo, ya, yb, yc):
    mask = low_half(N)

    def pair(mp, carry):
        for xk, wz, base in ((xkb, wzb, 0), (xka, wza, 128)):
            weights = wz[pl.ds(pl.multiple_of(mp * 256, 256), 256), 0:192]
            for q in range(4):
                z = dot_t(xk[q * 256 : (q + 1) * 256, 0:192], weights)
                hi, lo = split(z)
                for odd in range(2):
                    t_hi[odd * 1024 + q * 256 : odd * 1024 + (q + 1) * 256, base : base + 128] = hi[
                        :, odd * 128 : (odd + 1) * 128
                    ]
                    t_lo[odd * 1024 + q * 256 : odd * 1024 + (q + 1) * 256, base : base + 128] = lo[
                        :, odd * 128 : (odd + 1) * 128
                    ]
        for odd in range(2):
            m = mp * 2 + odd
            left = wy[m, :, 0:96]

            for i in range(N):
                at = slice(odd * 1024 + i * N, odd * 1024 + (i + 1) * N)
                hi, lo = t_hi[at, :], t_lo[at, :]
                y = dot(left, jnp.concatenate([hi, lo, hi], axis=0))
                to = pl.ds(m * N + i, N, stride=SIDE_LINE)
                ya[to, :] = y[:N, :128]
                yb[to, :] = y[:N, 128:]
                yc[to, :] = jnp.where(mask, y[N : 2 * N, :128], y[2 * N :, 128:])
        return carry

    lax.fori_loop(0, PAIRS, pair, 0)


def sides_columns(first_b, wx, wx0, ya, yb, yc, out):
    mask = low_half(N)

    def column(k, carry):
        at = pl.ds(pl.multiple_of((first_b + k) * SIDE_LINE, 8), TERMS * N)
        rows = pl.ds(pl.multiple_of(k * N, N), N)
        hi, lo = split(ya[at, :])
        first = dot(wx[0:128, :], hi)
        r = first[:64] + first[64:128] + dot(wx[0:64, :], lo)
        out[rows, 0:128] = jnp.where(mask, r[:N], r[N:])
        hi, lo = split(yb[at, :])
        first = dot(wx[128:256, :], hi)
        r = first[:64] + first[64:128] + dot(wx[128:192, :], lo)
        out[rows, 128:256] = jnp.where(mask, r[:N], r[N:])
        hi, lo = split(yc[at, :])
        first = dot(wx0[...], hi)
        out[rows, 256:384] = first[:N] + first[N:] + dot(wx0[0:N, :], lo)
        return carry

    lax.fori_loop(0, 8, column, 0, unroll=4)


def fold(f, hx, ht, folded, kron, mats):
    def row(a, carry):
        wide = hx[pl.ds(a, 1), :]
        for g in range(8):
            at = pl.ds(pl.multiple_of(g * 1024 + a * N, N), N)
            kron[at, :] = wide[:, g * 128 : (g + 1) * 128] * ht[...]
        return carry

    lax.fori_loop(0, N, row, 0, unroll=4)
    f_hi, f_lo = split(f[...])
    for n in range(4):
        left, right = split(kron[2048 * n : 2048 * n + 1024, :]), split(kron[2048 * n + 1024 : 2048 * n + 2048, :])
        hi, lo = jnp.concatenate([left[0], right[0]], axis=1), jnp.concatenate([left[1], right[1]], axis=1)
        folded[:, n * 256 : (n + 1) * 256] = dot(f_hi, hi) + dot(f_lo, hi) + dot(f_hi, lo)
    for g in range(8):
        piece = folded[:, g * 128 : (g + 1) * 128]
        for k in range(4):
            turned = piece if k == 0 else pltpu.roll(piece, 128 - 32 * k, 1)
            mats[pl.ds(4 * g + k, 192, stride=MAT_LINE), :] = turned


def pack(mats, wzo, wzb, wza, wys, wxo, wxs, wx0):
    mask = lax.broadcasted_iota(jnp.int32, (N, 128), 1) < N

    def matrix(m, axis, offset):
        start = (m * 9 + axis * 3 + offset) * MAT_LINE
        v = mats[pl.ds(start if isinstance(m, int) else pl.multiple_of(start, 8), N), :]
        return jnp.where(mask, v, 0.0)

    def parts(v):
        hi = v.astype(bf16).astype(f32)
        return hi, v - hi

    def term(m, carry):
        for t, offset in enumerate((1, 2, 0)):
            hi, lo = parts(matrix(m, 1, offset))
            wys[m, t * N : (t + 1) * N, :] = (hi + pltpu.roll(hi, 32, 1) + pltpu.roll(lo, 64, 1)).astype(bf16)
        for offset, places in ((0, ((wza, 0),)), (1, ((wzo, 0), (wzb, 0), (wza, 64))), (2, ((wzb, 64),))):
            hi, lo = parts(matrix(m, 2, offset))
            first = hi + pltpu.roll(hi, 64, 1)
            for ref, base in places:
                start = m * (64 if ref is wzo else 128) + base
                for p in range(2):
                    at = pl.ds(pl.multiple_of(start + p * N, N), N)
                    ref[at, 0:128] = (pltpu.roll(first, 32, 1) if p else first).astype(bf16)
                    ref[at, 128:256] = (pltpu.roll(lo, 32, 1) if p else lo).astype(bf16)
        return carry

    lax.fori_loop(0, TERMS, term, 0)

    def wide(terms, offset):
        total = None
        for k, m in enumerate(terms):
            v = matrix(m, 0, offset)
            v = pltpu.roll(v, 32 * k, 1) if k else v
            total = v if total is None else total + v
        return split(total)

    for g in range(5):
        at = slice(g * 128, (g + 1) * 128)
        for offset, places in ((2, ((wxs, 0, 64),)), (1, ((wxs, 32, 96), (wxs, 128, 192), (wx0, 0, 32))), (0, ((wxs, 160, 224),))):
            hi, lo = wide(range(4 * g, 4 * g + 4), offset)
            for ref, high_at, low_at in places:
                ref[high_at : high_at + N, at] = hi
                ref[low_at : low_at + N, at] = lo
    for g in range(3):
        at = slice(g * 128, (g + 1) * 128)
        for odd in range(2):
            hi, lo = wide([2 * mp + odd for mp in range(4 * g, min(4 * g + 4, PAIRS))], 1)
            wxo[odd * N : (odd + 1) * N, at] = hi
            wxo[64 + odd * N : 64 + (odd + 1) * N, at] = lo


MESH = pl.DeviceIdType.MESH
Y, CORES, ROWS = 4, 2, 16


def start_copy(src, dst, s, r, peer):
    copy = pltpu.make_async_remote_copy(
        src_ref=src, dst_ref=dst, send_sem=s, recv_sem=r, device_id=peer, device_id_type=MESH
    )
    copy.start()
    return copy


def greet(peers):
    barrier = pltpu.get_barrier_semaphore()
    for peer in peers:
        pl.semaphore_signal(barrier, inc=1, device_id=peer, device_id_type=MESH)
    pl.semaphore_wait(barrier, len(peers))


BOX_LINE = N + 8


def lay_out(boxes, lines, xs):
    piece = lax.broadcasted_iota(jnp.int32, (16, 128), 1) // 16

    def octant(at, carry):
        ox, oy, jh = at // 4, at // 2 % 2, at % 2
        rows = [boxes[p * 8 + ox * 4 + oy * 2 + oz, pl.ds(jh, 16, stride=2), :] for p in range(2) for oz in range(2)]
        for j in range(8):
            x = None
            for k in range(4):
                shift = (16 * (k - j)) % 128
                v = pltpu.roll(rows[k], shift, 1) if shift else rows[k]
                x = v if x is None else jnp.where(piece == k, v, x)
            lines[pl.ds(ox * 16 * BOX_LINE + oy * 16 + jh * 8 + j, 16, stride=BOX_LINE), :] = x
        return carry

    lax.fori_loop(0, 8, octant, 0)
    mask = low_half(N)

    def line(i, carry):
        v = lines[pl.ds(pl.multiple_of(i * BOX_LINE, 8), N), :]
        hi = v.astype(bf16).astype(f32)
        at = pl.ds(pl.multiple_of(i * N, N), N)
        xs[at, 0:128] = jnp.where(mask, hi, pltpu.roll(v - hi, 64, 1)).astype(bf16)
        xs[at, 128:256] = v.astype(bf16)
        return carry

    lax.fori_loop(0, N, line, 0, unroll=4)


def own_lanes(v, core):
    return jnp.where(core == 1, pltpu.roll(v, 64, 1), v)


def lay_back(applied, boxes):
    piece = lax.broadcasted_iota(jnp.int32, (16, 128), 1) // 16

    def octants(at, carry):
        ox, oy, jh = at // 4, at // 2 % 2, at % 2
        start = (oy * 16 + jh * 8) * N + ox * 16
        lines = [applied[pl.ds(pl.multiple_of(start + j * N, 16), 16), :] for j in range(8)]
        for p in range(2):
            for oz in range(2):
                box = None
                for j in range(8):
                    shift = (16 * j - p * 32 - oz * 16) % 128
                    v = pltpu.roll(lines[j], shift, 1) if shift else lines[j]
                    box = v if box is None else jnp.where(piece == j, v, box)
                boxes[p * 8 + ox * 4 + oy * 2 + oz, pl.ds(jh, 16, stride=2), :] = box
        return carry

    lax.fori_loop(0, 8, octants, 0)


def convolve_kernel(fine, tags, source, slot, f, hx, ht, hit, out,
                    wzo, wzb, wza, wys, wxo, wxs, wx0, sel, folded, leaving, arrived, boxes, lines, xs,
                    t_hi, t_lo, ya, yb, yc, terms, part, centre, from_core, pair_sum, from_y, total,
                    from_half, returned, back, s1, r1, s2, r2, s3, r3, s4, r4, s5, r5, s6, r6):
    row, col = lax.axis_index("row"), lax.axis_index("col")
    y, core = col // CORES, col % CORES
    sibling = (row, y * CORES + (1 - core))
    across = [(row, (y + 1 + d) % Y * CORES + core) for d in range(Y - 1)]
    greet([sibling] + across + [((row + d) % ROWS, col) for d in range(1, ROWS)])

    arrivals = []
    for d in list(range(1, ROWS)) + [0]:
        to = (row + d) % ROWS
        target = arrived.at[row] if d == 0 else leaving.at[d]
        target[0:32, :] = fine[source[2 * to]]
        target[32:64, :] = fine[source[2 * to + 1]]
        target[64:72, :] = tags[to]
        if d:
            arrivals.append(start_copy(leaving.at[d], arrived.at[row], s1.at[d], r1.at[d], (to, col)))
    fold(f, hx, ht, folded, yb, ya)
    for copy in arrivals:
        copy.wait_recv()

    def place(at, carry):
        wanted = at.astype(f32)
        total = [jnp.zeros((8, 128), f32)] * 4
        for k in range(ROWS):
            for s in range(2):
                hit = jnp.broadcast_to(arrived[k, 64 + s : 65 + s, :], (8, 128)) == wanted
                for c in range(4):
                    start = s * 32 + c * 8
                    total[c] = jnp.where(hit, arrived[k, start : start + 8, :], total[c])
        for c in range(4):
            boxes[0, at, c * 8 : (c + 1) * 8, :] = total[c]
        return carry

    lax.fori_loop(0, 16, place, 0)

    hops = [
        start_copy(boxes.at[0], boxes.at[1], s2.at[0], r2.at[0], ((row + 1) % ROWS, col)),
        start_copy(boxes.at[0], boxes.at[2], s2.at[1], r2.at[1], ((row + ROWS - 1) % ROWS, col)),
    ]
    pack(ya, wzo, wzb, wza, wys, wxo, wxs, wx0)
    same = lax.broadcasted_iota(jnp.int32, (N, 512), 1) % N == lax.broadcasted_iota(jnp.int32, (N, 512), 0)
    for k in range(12):
        sel[k * N : (k + 1) * N, :] = jnp.where(same, hit[k : k + 1, :], 0.0).astype(bf16)
    lay_out(boxes.at[0], lines, xs.at[0])
    for hop, k in zip(hops, (1, 2)):
        hop.wait_recv()
        lay_out(boxes.at[k], lines, xs.at[k])

    sides_lines(xs.at[1], xs.at[2], wzb, wza, wys, t_hi, t_lo, ya, yb, yc)
    mine = pl.ds(pl.multiple_of(core * 128, 128), 128)
    other = pl.ds(pl.multiple_of((1 - core) * 128, 128), 128)
    pairs, sums = [], []

    def over_pair(c):
        pairs[c].wait_recv()
        for d in range(Y):
            to = (y + 1 + d) % Y
            v = part[c, to, mine, :] + from_core[c, to]
            if d < Y - 1:
                pair_sum[c, d] = v
                k = c * (Y - 1) + d
                sums.append(start_copy(pair_sum.at[c, d], from_y.at[c, d], s4.at[k], r4.at[k], across[d]))
            else:
                total[c] = v

    for c in range(4):
        sides_columns(8 * c, wxs, wx0, ya, yb, yc, terms)
        hi, lo = split(terms[...])
        summed = dot(hi, sel[...]) + dot(lo, sel[...])
        for k in range(Y):
            part[c, k] = summed[:, k * 128 : (k + 1) * 128]
        pairs.append(start_copy(part.at[c, :, other], from_core.at[c], s3.at[c], r3.at[c], sibling))
        if c:
            over_pair(c - 1)
    over_pair(3)
    centre_pass(xs.at[0], wzo, wys, wxo, t_hi, t_lo, ya, centre)
    halves = []
    for c in range(4):
        for d in range(Y - 1):
            sums[c * (Y - 1) + d].wait_recv()
        total[c] = total[c] + from_y[c, 0] + from_y[c, 1] + from_y[c, 2]
        halves.append(start_copy(total.at[c], from_half.at[c], s5.at[c], r5.at[c], sibling))
    for c in range(4):
        at = pl.ds(pl.multiple_of(c * 256 + core * 128, 128), 128)
        centre[at, :] = centre[at, :] + own_lanes(total[c], core)
    for c in range(4):
        halves[c].wait_recv()
        at = pl.ds(pl.multiple_of(c * 256 + (1 - core) * 128, 128), 128)
        centre[at, :] = centre[at, :] + own_lanes(from_half[c], core)

    result = boxes.at[0]
    for hop in hops:
        hop.wait_send()
    lay_back(centre, result)

    def give_back(d, carry):
        to = (row + d) % ROWS
        for s in range(2):
            place = jnp.broadcast_to(arrived[to, pl.ds(64 + s, 1), :], (8, 128))
            hit = [place == float(k) for k in range(16)]
            for c in range(4):
                rows = slice(c * 8, (c + 1) * 8)
                v = result[0, rows, :]
                for k in range(1, 16):
                    v = jnp.where(hit[k], result[k, rows, :], v)
                returned[d * 2 + s, rows, :] = v
        return carry

    lax.fori_loop(0, ROWS, give_back, 0)
    returns = []
    for d in range(1, ROWS):
        src, dst = returned.at[pl.ds(2 * d, 2)], back.at[pl.ds(row * 2, 2)]
        returns.append(start_copy(src, dst, s6.at[d], r6.at[d], ((row + d) % ROWS, col)))
    for s in range(2):
        back[row * 2 + s] = returned[s]
    for copy in returns:
        copy.wait_recv()
    for q in range(16):
        out[q] = back[slot[q]]
    for copy in arrivals + pairs + sums + halves + returns:
        copy.wait_send()


def convolve(fine, tags, source, slot, filter_matrix, kernel_ops, hit):
    f = jnp.pad(kernel_ops.reshape(TERMS * 9, N * N), ((0, 12), (0, 0)))
    hx = jnp.repeat(filter_matrix, N, axis=1)
    ht = jnp.tile(filter_matrix, (1, 4))
    vm = pl.BlockSpec(memory_space=pltpu.VMEM)
    sm = pl.BlockSpec(memory_space=pltpu.SMEM)
    low = ((1280, 256), (2560, 256), (2560, 256), (TERMS, 96, 128), (128, 384), (256, 640), (64, 640), (384, 512))
    scratch = [pltpu.VMEM(shape, bf16) for shape in low]
    scratch += [pltpu.VMEM(shape, f32) for shape in ((192, 1024), (16, 72, 128), (16, 72, 128), (3, 16, 32, 128), (N * BOX_LINE, 128))]
    scratch += [pltpu.VMEM(shape, bf16) for shape in ((3, 1024, 256), (2048, 256), (2048, 256))]
    scratch += [pltpu.VMEM((N * SIDE_LINE, 128), f32)] * 3
    scratch += [
        pltpu.VMEM(shape, f32)
        for shape in (
            (256, 384), (4, 4, 256, 128), (1024, 128), (4, 4, 128, 128), (4, 3, 128, 128), (4, 3, 128, 128),
            (4, 128, 128), (4, 128, 128), (32, 32, 128), (32, 32, 128),
        )
    ]
    scratch += [pltpu.SemaphoreType.DMA((n,)) for n in (16, 16, 2, 2, 4, 4, 12, 12, 4, 4, 16, 16)]
    return pl.pallas_call(
        convolve_kernel,
        out_shape=jax.ShapeDtypeStruct((16, 32, 128), f32),
        in_specs=[vm, vm, sm, sm, vm, vm, vm, vm],
        out_specs=vm,
        scratch_shapes=scratch,
        compiler_params=pltpu.CompilerParams(
            collective_id=1, has_side_effects=True, vmem_limit_bytes=60 * 2**20
        ),
    )(fine, tags, source, slot, f, hx, ht, hit)


def hits(neighbours, col_index):
    order = (1, 5, 4, 0, 3, 2)
    sender = jnp.stack([neighbours[:, k] for k in order for p in range(2)])
    parent = (jnp.arange(12) % 2)[:, None] + col_index * 2
    hit = ((sender >= 0) & (sender % 16 == parent)).astype(f32)
    return jnp.repeat(hit, N, axis=1)


def local(fine_coeffs, fine_slot, neighbours, filter_matrix, kernel_ops):
    held_boxes, volume = fine_coeffs.shape
    dest_row = fine_slot // 128
    item = jnp.arange(held_boxes)
    earlier = (dest_row[None, :] == dest_row[:, None]) & (item[None, :] < item[:, None])
    slot_index = dest_row * 2 + jnp.sum(earlier.astype(jnp.int32), axis=1)
    packer = jnp.arange(2 * ROWS)[:, None] == slot_index[None, :]
    source = jnp.sum(jnp.where(packer, item[None, :], 0), axis=1)
    places = jnp.max(jnp.where(packer, fine_slot[None, :] % 16, -1), axis=1).astype(f32)
    tags = jnp.broadcast_to(places.reshape(ROWS, 2, 1), (ROWS, 2, 128))
    tags = jnp.pad(tags, ((0, 0), (0, 6), (0, 0)))
    boxes = fine_coeffs.reshape(held_boxes, 32, 128)
    hit = hits(neighbours, lax.axis_index("col"))
    out = convolve(boxes, tags, source, slot_index, filter_matrix, kernel_ops, hit)
    return out.reshape(held_boxes, volume)


def solution(mesh):
    in_specs = (P(("row", "col"), None), P(("row", "col")), P("row", None), P(), P())
    out_specs = P(("row", "col"), None)
    return jax.shard_map(local, mesh=mesh, in_specs=in_specs, out_specs=out_specs, check_vma=False)
```

time: 114 us -> 87.4 us (0.77)
  Pallas kernels: 94.8 us -> 74.7 us
  local copies, waits for them, and re-layouts: 17.3 us -> 10.5 us
    pallas_call x3 -> x1, Pallas kernels: 94.8 us -> 74.7 us  [convolve(): pl.pallas_call(convolve_kernel, out_shape=jax.ShapeDtypeStruct((16, 32, 1...]
    unnamed x27 -> x11, local copies, waits for them, and re-layouts: 12 us -> 4.86 us
    mul x1 -> x0, local copies, waits for them, and re-layouts: 2.3 us -> none  [selection(): hit[:, :, None, :, None] * jnp.eye(N, dtype=bf16)[None, None, :, None, :]]
    reshape x2 -> x3, local copies, waits for them, and re-layouts: 0.61 us -> 1.94 us  [the longest x1 0.88 us: convolve(): hx = jnp.repeat(filter_matrix, N, axis=1)]
where the time goes in v2:
time: 87.4 us; the launch traced here: 86.2 us
  Pallas kernels  74.7 us (85%)
  local copies, waits for them, and re-layouts  10.5 us (12%)
  other arithmetic  0.96 us (1%)
    pallas_call x1, Pallas kernels, convolve(): pl.pallas_call(convolve_kernel, out_shape=jax.ShapeDtypeStruct((16, 32, 1...  74.7 us
    unnamed x11, local copies, waits for them, and re-layouts  4.86 us

profile of v2, /device:TPU:0, one launch (start us, length us, event | category | flops | bytes accessed | tf_op | source)
XLA Modules:
  0.0 86.2 jit_solution(11781245401128945374)
XLA Ops:
  0.0 0.9 %slice_bitcast_fusion = (s32[1,16]{1,0:T(1,128)S(1)}, s32[1,16]{1,0:T(1,128)S(1)}, s32[1,16]{1,0:T(1,128)S(1)}, s32[1,16]{1,0:T(1,128)S(1)}, s32[1,16]{1,0:T(1,128)S(1)}, /*index=5*/s32[1,16]{1,0:T(1,128)S(1)}) fusion(s32[16,6]{0,1:T(8,128)} %param.7), kind=kLoop, calls=%fused_computation.22 | loop fusion | bytes 768 | tf_op jit(solution)/shard_map/stack;squeeze | solution.py:424
  1.0 0.1 fusion.4
  1.0 0.1 broadcast_in_dim.46
  1.1 0.0 copy-start.3
  1.1 0.7 reshape.50.hit
  1.8 0.0 copy-done.3
  1.9 0.2 convert_reduce_fusion
  2.0 0.0 copy-start.2
  2.0 0.5 copy-done.2
  2.6 0.7 select_reduce_fusion
  3.3 0.1 convert_element_type.22
  3.4 0.1 broadcast_in_dim.42
  3.4 0.6 pad.8.tags
  4.1 1.7 %copy.8 = f32[20,3,3,1024]{3,2,1,0:T(4,128)S(1)} copy(f32[20,3,3,1024]{3,0,2,1:T(8,128)} %param.9) | data formatting | bytes 1474560 | tf_op args[4]
  5.8 0.4 reshape.48
  6.1 0.0 copy-start.1
  6.1 0.9 %pad.9.f = f32[192,1024]{1,0:T(8,128)} pad(f32[180,1024]{1,0:T(8,128)S(1)} %reshape.48, f32[]{:T(128)} %constant.62.clone.1), padding=0_12x0_0 | pad | bytes 1523716 | tf_op jit(solution)/shard_map/jit(_pad)/pad | solution.py:392
  7.1 0.0 copy-done.1
  7.1 0.2 broadcast_in_dim.45
  7.3 0.0 copy-start
  7.3 0.9 %reshape.49.hx = f32[32,1024]{1,0:T(8,128)} reshape(f32[32,32,32]{2,1,0:T(8,128)S(1)} %broadcast_in_dim.45) | data formatting | bytes 262144 | tf_op jit(solution)/shard_map/reshape | solution.py:393
  8.2 0.1 copy-done
  8.2 0.8 copy.9
  9.0 0.7 tile.10.ht
  9.7 74.7 %shard_map.55 = f32[16,32,128]{2,1,0:T(8,128)} custom-call(f32[16,32,128]{2,1,0:T(8,128)} %bitcast.18, f32[16,8,128]{2,1,0:T(8,128)} %pad.8.tags, s32[32]{0:T(128)} %get-tuple-element.5.source, s32[16]{0:T(128)} %copy-done.2, f32[192,1024]{1,0:T(8,128)} %pad.9.f, f32[32,1024]{1,0:T(8,128)} %reshape.49.hx, f32[32,128]{1,0:T(8,128)} %tile.10.ht, ...), custom_call_target="tpu_custom_call" | custom-call | tf_op jit(solution)/shard_map/pallas_call | solution.py:410
  84.4 1.8 %copy.12 = f32[2,8,32,128]{3,1,2,0:T(8,128)} copy(f32[2,8,32,128]{3,2,1,0:T(8,128)} %bitcast.19) | data formatting | bytes 524288
  (6 shorter events, 0.1 us)
Async XLA Ops:
  1.1 0.7 copy-start.3
  2.0 0.5 copy-start.2
  6.1 1.0 %copy-start.1 = (f32[32,32]{1,0:T(8,128)S(1)}, f32[32,32]{1,0:T(8,128)}, u32[]{:S(2)}) copy-start(f32[32,32]{1,0:T(8,128)} %param.8) | copy-start | bytes 12292
  7.3 1.0 %copy-start = (f32[16,4096]{1,0:T(8,128)S(1)}, f32[16,4096]{1,0:T(8,128)}, u32[]{:S(2)}) copy-start(f32[16,4096]{1,0:T(8,128)} %param.5) | copy-start | bytes 786436

commit v3 on v2

--- a/solution.py
+++ b/solution.py
@@ -114,7 +114,22 @@
     lax.fori_loop(0, 8, column, 0, unroll=4)
 
 
-def fold(f, hx, ht, folded, kron, mats):
+def spread(h, lanes, pick):
+    shape = (N, lanes)
+    chosen = pick(lax.broadcasted_iota(jnp.int32, shape, 1)) == lax.broadcasted_iota(jnp.int32, shape, 0)
+    chosen = jnp.where(chosen, 1.0, 0.0).astype(bf16)
+    hi = split(h)[0]
+    mid, low = split(h - hi.astype(f32))
+    return dot(hi, chosen) + (dot(mid, chosen) + dot(low, chosen))
+
+
+def fold(ops, h, f, hx, ht, folded, kron, mats):
+    for k in range(9):
+        f[k * 24 : k * 24 + TERMS, :] = ops[k // 3, k % 3]
+        f[k * 24 + TERMS : (k + 1) * 24, :] = jnp.zeros((4, 1024), f32)
+    hx[...] = spread(h[...], 1024, lambda lane: lane // N)
+    ht[...] = spread(h[...], 128, lambda lane: lane % N)
+
     def row(a, carry):
         wide = hx[pl.ds(a, 1), :]
         for g in range(8):
@@ -132,14 +147,14 @@
         piece = folded[:, g * 128 : (g + 1) * 128]
         for k in range(4):
             turned = piece if k == 0 else pltpu.roll(piece, 128 - 32 * k, 1)
-            mats[pl.ds(4 * g + k, 192, stride=MAT_LINE), :] = turned
+            mats[pl.ds(4 * g + k, 216, stride=MAT_LINE), :] = turned
 
 
 def pack(mats, wzo, wzb, wza, wys, wxo, wxs, wx0):
     mask = lax.broadcasted_iota(jnp.int32, (N, 128), 1) < N
 
     def matrix(m, axis, offset):
-        start = (m * 9 + axis * 3 + offset) * MAT_LINE
+        start = ((axis * 3 + offset) * 24 + m) * MAT_LINE
         v = mats[pl.ds(start if isinstance(m, int) else pl.multiple_of(start, 8), N), :]
         return jnp.where(mask, v, 0.0)
 
@@ -238,10 +253,6 @@
     lax.fori_loop(0, N, line, 0, unroll=4)
 
 
-def own_lanes(v, core):
-    return jnp.where(core == 1, pltpu.roll(v, 64, 1), v)
-
-
 def lay_back(applied, boxes):
     piece = lax.broadcasted_iota(jnp.int32, (16, 128), 1) // 16
 
@@ -262,26 +273,53 @@
     lax.fori_loop(0, 8, octants, 0)
 
 
-def convolve_kernel(fine, tags, source, slot, f, hx, ht, hit, out,
+def choose(neighbours, col, sel):
+    lane = lax.broadcasted_iota(jnp.int32, (N, 128), 1)
+    same = lane % N == lax.broadcasted_iota(jnp.int32, (N, 128), 0)
+    for d, k in enumerate((1, 5, 4, 0, 3, 2)):
+        for g in range(4):
+            held = None
+            for n in range(4):
+                sender = neighbours[k, (g % 2 * 2 + n // 2) * 4 + g // 2 * 2 + n % 2]
+                v = jnp.where(sender >= 0, sender % 16 - 2 * col, -1)
+                held = v if held is None else jnp.where(lane // N == n, v, held)
+            for p in range(2):
+                at = slice((d * 2 + p) * N, (d * 2 + p + 1) * N)
+                sel[at, g * 128 : (g + 1) * 128] = jnp.where(same & (held == p), 1.0, 0.0).astype(bf16)
+
+
+def convolve_kernel(fine, slot, neighbours, ops, h, out, own, f, hx, ht,
                     wzo, wzb, wza, wys, wxo, wxs, wx0, sel, folded, leaving, arrived, boxes, lines, xs,
                     t_hi, t_lo, ya, yb, yc, terms, part, centre, from_core, pair_sum, from_y, total,
-                    from_half, returned, back, s1, r1, s2, r2, s3, r3, s4, r4, s5, r5, s6, r6):
+                    returned, back, s1, r1, s2, r2, s3, r3, s4, r4, s6, r6):
     row, col = lax.axis_index("row"), lax.axis_index("col")
     y, core = col // CORES, col % CORES
     sibling = (row, y * CORES + (1 - core))
     across = [(row, (y + 1 + d) % Y * CORES + core) for d in range(Y - 1)]
     greet([sibling] + across + [((row + d) % ROWS, col) for d in range(1, ROWS)])
 
+    for q in range(16):
+        own[q] = fine[pl.ds(q // 8 * 256 + q % 8, N, stride=8), :]
+    slots = [slot[q] for q in range(16)]
+    dest = [v // 128 for v in slots]
+    first_row = lax.broadcasted_iota(jnp.int32, (8, 128), 0) == 0
     arrivals = []
     for d in list(range(1, ROWS)) + [0]:
         to = (row + d) % ROWS
         target = arrived.at[row] if d == 0 else leaving.at[d]
-        target[0:32, :] = fine[source[2 * to]]
-        target[32:64, :] = fine[source[2 * to + 1]]
-        target[64:72, :] = tags[to]
+        first, last = jnp.int32(16), jnp.int32(-1)
+        for q in range(16):
+            here = dest[q] == to
+            first = jnp.minimum(first, jnp.where(here, q, 16))
+            last = jnp.maximum(last, jnp.where(here, q, -1))
+        tag = []
+        for k, q in enumerate((jnp.minimum(first, 15), jnp.maximum(last, 0))):
+            target[k * N : (k + 1) * N, :] = own[q]
+            tag.append(jnp.where(last >= 0, slot[q] % 16, -1).astype(f32))
+        target[64:72, :] = jnp.where(first_row, tag[0], tag[1])
         if d:
             arrivals.append(start_copy(leaving.at[d], arrived.at[row], s1.at[d], r1.at[d], (to, col)))
-    fold(f, hx, ht, folded, yb, ya)
+    fold(ops, h, f, hx, ht, folded, yb, ya)
     for copy in arrivals:
         copy.wait_recv()
 
@@ -305,24 +343,25 @@
         start_copy(boxes.at[0], boxes.at[2], s2.at[1], r2.at[1], ((row + ROWS - 1) % ROWS, col)),
     ]
     pack(ya, wzo, wzb, wza, wys, wxo, wxs, wx0)
-    same = lax.broadcasted_iota(jnp.int32, (N, 512), 1) % N == lax.broadcasted_iota(jnp.int32, (N, 512), 0)
-    for k in range(12):
-        sel[k * N : (k + 1) * N, :] = jnp.where(same, hit[k : k + 1, :], 0.0).astype(bf16)
+    choose(neighbours, col, sel)
     lay_out(boxes.at[0], lines, xs.at[0])
     for hop, k in zip(hops, (1, 2)):
         hop.wait_recv()
         lay_out(boxes.at[k], lines, xs.at[k])
 
     sides_lines(xs.at[1], xs.at[2], wzb, wza, wys, t_hi, t_lo, ya, yb, yc)
-    mine = pl.ds(pl.multiple_of(core * 128, 128), 128)
-    other = pl.ds(pl.multiple_of((1 - core) * 128, 128), 128)
     pairs, sums = [], []
+    mask = low_half(128)
 
     def over_pair(c):
         pairs[c].wait_recv()
         for d in range(Y):
             to = (y + 1 + d) % Y
-            v = part[c, to, mine, :] + from_core[c, to]
+            v = part[c, core, to // 2] + from_core[c, to // 2]
+            odd = to % 2 == 1
+            low = jnp.where(odd, pltpu.roll(v[:128], 64, 1), v[:128])
+            high = jnp.where(odd, v[128:], pltpu.roll(v[128:], 64, 1))
+            v = jnp.where(mask, low, high)
             if d < Y - 1:
                 pair_sum[c, d] = v
                 k = c * (Y - 1) + d
@@ -335,25 +374,20 @@
         hi, lo = split(terms[...])
         summed = dot(hi, sel[...]) + dot(lo, sel[...])
         for k in range(Y):
-            part[c, k] = summed[:, k * 128 : (k + 1) * 128]
-        pairs.append(start_copy(part.at[c, :, other], from_core.at[c], s3.at[c], r3.at[c], sibling))
+            part[c, k // 2, k % 2] = summed[:, k * 128 : (k + 1) * 128]
+        pairs.append(start_copy(part.at[c, 1 - core], from_core.at[c], s3.at[c], r3.at[c], sibling))
         if c:
             over_pair(c - 1)
     over_pair(3)
     centre_pass(xs.at[0], wzo, wys, wxo, t_hi, t_lo, ya, centre)
-    halves = []
     for c in range(4):
         for d in range(Y - 1):
             sums[c * (Y - 1) + d].wait_recv()
-        total[c] = total[c] + from_y[c, 0] + from_y[c, 1] + from_y[c, 2]
-        halves.append(start_copy(total.at[c], from_half.at[c], s5.at[c], r5.at[c], sibling))
-    for c in range(4):
-        at = pl.ds(pl.multiple_of(c * 256 + core * 128, 128), 128)
-        centre[at, :] = centre[at, :] + own_lanes(total[c], core)
-    for c in range(4):
-        halves[c].wait_recv()
-        at = pl.ds(pl.multiple_of(c * 256 + (1 - core) * 128, 128), 128)
-        centre[at, :] = centre[at, :] + own_lanes(from_half[c], core)
+        v = total[c] + from_y[c, 0] + from_y[c, 1] + from_y[c, 2]
+        at = slice(c * 256, c * 256 + 128)
+        centre[at, :] = centre[at, :] + v
+        at = slice(c * 256 + 128, c * 256 + 256)
+        centre[at, :] = centre[at, :] + pltpu.roll(v, 64, 1)
 
     result = boxes.at[0]
     for hop in hops:
@@ -383,65 +417,48 @@
     for copy in returns:
         copy.wait_recv()
     for q in range(16):
-        out[q] = back[slot[q]]
-    for copy in arrivals + pairs + sums + halves + returns:
+        earlier = jnp.int32(0)
+        for k in range(q):
+            earlier = jnp.where(dest[k] == dest[q], 1, earlier)
+        out[pl.ds(q // 8 * 256 + q % 8, N, stride=8), :] = back[2 * dest[q] + earlier]
+    for copy in arrivals + pairs + sums + returns:
         copy.wait_send()
 
 
-def convolve(fine, tags, source, slot, filter_matrix, kernel_ops, hit):
-    f = jnp.pad(kernel_ops.reshape(TERMS * 9, N * N), ((0, 12), (0, 0)))
-    hx = jnp.repeat(filter_matrix, N, axis=1)
-    ht = jnp.tile(filter_matrix, (1, 4))
+def convolve(fine, slot, neighbours, kernel_ops, filter_matrix):
     vm = pl.BlockSpec(memory_space=pltpu.VMEM)
     sm = pl.BlockSpec(memory_space=pltpu.SMEM)
     low = ((1280, 256), (2560, 256), (2560, 256), (TERMS, 96, 128), (128, 384), (256, 640), (64, 640), (384, 512))
-    scratch = [pltpu.VMEM(shape, bf16) for shape in low]
-    scratch += [pltpu.VMEM(shape, f32) for shape in ((192, 1024), (16, 72, 128), (16, 72, 128), (3, 16, 32, 128), (N * BOX_LINE, 128))]
+    scratch = [pltpu.VMEM(shape, f32) for shape in ((16, 32, 128), (216, 1024), (32, 1024), (32, 128))]
+    scratch += [pltpu.VMEM(shape, bf16) for shape in low]
+    scratch += [pltpu.VMEM(shape, f32) for shape in ((216, 1024), (16, 72, 128), (16, 72, 128), (3, 16, 32, 128), (N * BOX_LINE, 128))]
     scratch += [pltpu.VMEM(shape, bf16) for shape in ((3, 1024, 256), (2048, 256), (2048, 256))]
     scratch += [pltpu.VMEM((N * SIDE_LINE, 128), f32)] * 3
     scratch += [
         pltpu.VMEM(shape, f32)
         for shape in (
-            (256, 384), (4, 4, 256, 128), (1024, 128), (4, 4, 128, 128), (4, 3, 128, 128), (4, 3, 128, 128),
-            (4, 128, 128), (4, 128, 128), (32, 32, 128), (32, 32, 128),
+            (256, 384), (4, 2, 2, 256, 128), (1024, 128), (4, 2, 256, 128), (4, 3, 128, 128), (4, 3, 128, 128),
+            (4, 128, 128), (32, 32, 128), (32, 32, 128),
         )
     ]
-    scratch += [pltpu.SemaphoreType.DMA((n,)) for n in (16, 16, 2, 2, 4, 4, 12, 12, 4, 4, 16, 16)]
+    scratch += [pltpu.SemaphoreType.DMA((n,)) for n in (16, 16, 2, 2, 4, 4, 12, 12, 16, 16)]
     return pl.pallas_call(
         convolve_kernel,
-        out_shape=jax.ShapeDtypeStruct((16, 32, 128), f32),
-        in_specs=[vm, vm, sm, sm, vm, vm, vm, vm],
+        out_shape=jax.ShapeDtypeStruct((512, 128), f32),
+        in_specs=[vm, sm, sm, vm, vm],
         out_specs=vm,
         scratch_shapes=scratch,
         compiler_params=pltpu.CompilerParams(
             collective_id=1, has_side_effects=True, vmem_limit_bytes=60 * 2**20
         ),
-    )(fine, tags, source, slot, f, hx, ht, hit)
-
-
-def hits(neighbours, col_index):
-    order = (1, 5, 4, 0, 3, 2)
-    sender = jnp.stack([neighbours[:, k] for k in order for p in range(2)])
-    parent = (jnp.arange(12) % 2)[:, None] + col_index * 2
-    hit = ((sender >= 0) & (sender % 16 == parent)).astype(f32)
-    return jnp.repeat(hit, N, axis=1)
+    )(fine, slot, neighbours, kernel_ops, filter_matrix)
 
 
 def local(fine_coeffs, fine_slot, neighbours, filter_matrix, kernel_ops):
     held_boxes, volume = fine_coeffs.shape
-    dest_row = fine_slot // 128
-    item = jnp.arange(held_boxes)
-    earlier = (dest_row[None, :] == dest_row[:, None]) & (item[None, :] < item[:, None])
-    slot_index = dest_row * 2 + jnp.sum(earlier.astype(jnp.int32), axis=1)
-    packer = jnp.arange(2 * ROWS)[:, None] == slot_index[None, :]
-    source = jnp.sum(jnp.where(packer, item[None, :], 0), axis=1)
-    places = jnp.max(jnp.where(packer, fine_slot[None, :] % 16, -1), axis=1).astype(f32)
-    tags = jnp.broadcast_to(places.reshape(ROWS, 2, 1), (ROWS, 2, 128))
-    tags = jnp.pad(tags, ((0, 0), (0, 6), (0, 0)))
-    boxes = fine_coeffs.reshape(held_boxes, 32, 128)
-    hit = hits(neighbours, lax.axis_index("col"))
-    out = convolve(boxes, tags, source, slot_index, filter_matrix, kernel_ops, hit)
-    return out.reshape(held_boxes, volume)
+    boxes = jnp.transpose(fine_coeffs.reshape(2, 8, 32, 128), (0, 2, 1, 3)).reshape(512, 128)
+    out = convolve(boxes, fine_slot, neighbours.T, jnp.transpose(kernel_ops, (1, 2, 0, 3)), filter_matrix)
+    return jnp.transpose(out.reshape(2, 32, 8, 128), (0, 2, 1, 3)).reshape(held_boxes, volume)
 
 
 def solution(mesh):

time: 87.4 us -> 78 us (0.89)
  local copies, waits for them, and re-layouts: 10.5 us -> 1.67 us
  other arithmetic: 0.96 us -> 0 us
    unnamed x11 -> x1, local copies, waits for them, and re-layouts: 4.86 us -> 1.67 us
    reshape x3 -> x0, local copies, waits for them, and re-layouts: 1.94 us -> none  [the longest x1 0.88 us: convolve(): hx = jnp.repeat(filter_matrix, N, axis=1)]
    another operation x4 -> x0, local copies, waits for them, and re-layouts: 1.67 us -> none  [the longest x2 0.96 us: hits(): sender = jnp.stack([neighbours[:, k] for k in order for p in range(2)])]
    pad x2 -> x0, local copies, waits for them, and re-layouts: 1.59 us -> none  [the longest x1 0.94 us: convolve(): f = jnp.pad(kernel_ops.reshape(TERMS * 9, N * N), ((0, 12), (0, 0)))]
where the time goes in v3:
time: 78 us; the launch traced here: 76.8 us
  Pallas kernels  75.1 us (96%)
  local copies, waits for them, and re-layouts  1.67 us (2%)
    pallas_call x1, Pallas kernels, convolve(): pl.pallas_call(convolve_kernel, out_shape=jax.ShapeDtypeStruct((512, 128)...  75.1 us
    unnamed x1, local copies, waits for them, and re-layouts  1.67 us

profile of v3, /device:TPU:0, one launch (start us, length us, event | category | flops | bytes accessed | tf_op | source)
XLA Modules:
  0.0 76.8 jit_solution(15337070084884568888)
XLA Ops:
  0.0 75.1 %shard_map.55 = f32[512,128]{1,0:T(8,128)} custom-call(f32[512,128]{1,0:T(8,128)} %bitcast.14, s32[16]{0:T(128)} %slot.1, s32[6,16]{1,0:T(8,128)} %bitcast.15, f32[3,3,20,1024]{3,2,1,0:T(8,128)} %bitcast.13, f32[32,32]{1,0:T(8,128)} %h.1), custom_call_target="tpu_custom_call" | custom-call | tf_op jit(solution)/shard_map/pallas_call | solution.py:445
  75.1 1.7 %copy.7 = f32[16,4096]{1,0:T(8,128)} copy(f32[16,4096]{1,0:T(8,128)} %bitcast.12) | data formatting | bytes 524288

commit v4 on v3

--- a/solution.py
+++ b/solution.py
@@ -214,13 +214,6 @@
     return copy
 
 
-def greet(peers):
-    barrier = pltpu.get_barrier_semaphore()
-    for peer in peers:
-        pl.semaphore_signal(barrier, inc=1, device_id=peer, device_id_type=MESH)
-    pl.semaphore_wait(barrier, len(peers))
-
-
 BOX_LINE = N + 8
 
 
@@ -239,7 +232,7 @@
             lines[pl.ds(ox * 16 * BOX_LINE + oy * 16 + jh * 8 + j, 16, stride=BOX_LINE), :] = x
         return carry
 
-    lax.fori_loop(0, 8, octant, 0)
+    lax.fori_loop(0, 8, octant, 0, unroll=4)
     mask = low_half(N)
 
     def line(i, carry):
@@ -250,7 +243,7 @@
         xs[at, 128:256] = v.astype(bf16)
         return carry
 
-    lax.fori_loop(0, N, line, 0, unroll=4)
+    lax.fori_loop(0, N, line, 0, unroll=8)
 
 
 def lay_back(applied, boxes):
@@ -270,7 +263,7 @@
                 boxes[p * 8 + ox * 4 + oy * 2 + oz, pl.ds(jh, 16, stride=2), :] = box
         return carry
 
-    lax.fori_loop(0, 8, octants, 0)
+    lax.fori_loop(0, 8, octants, 0, unroll=2)
 
 
 def choose(neighbours, col, sel):
@@ -296,15 +289,17 @@
     y, core = col // CORES, col % CORES
     sibling = (row, y * CORES + (1 - core))
     across = [(row, (y + 1 + d) % Y * CORES + core) for d in range(Y - 1)]
-    greet([sibling] + across + [((row + d) % ROWS, col) for d in range(1, ROWS)])
+    peers = [sibling] + across + [((row + d) % ROWS, col) for d in range(1, ROWS)]
+    barrier = pltpu.get_barrier_semaphore()
+    for peer in peers:
+        pl.semaphore_signal(barrier, inc=1, device_id=peer, device_id_type=MESH)
 
     for q in range(16):
         own[q] = fine[pl.ds(q // 8 * 256 + q % 8, N, stride=8), :]
     slots = [slot[q] for q in range(16)]
     dest = [v // 128 for v in slots]
     first_row = lax.broadcasted_iota(jnp.int32, (8, 128), 0) == 0
-    arrivals = []
-    for d in list(range(1, ROWS)) + [0]:
+    for d in range(ROWS):
         to = (row + d) % ROWS
         target = arrived.at[row] if d == 0 else leaving.at[d]
         first, last = jnp.int32(16), jnp.int32(-1)
@@ -317,36 +312,42 @@
             target[k * N : (k + 1) * N, :] = own[q]
             tag.append(jnp.where(last >= 0, slot[q] % 16, -1).astype(f32))
         target[64:72, :] = jnp.where(first_row, tag[0], tag[1])
-        if d:
-            arrivals.append(start_copy(leaving.at[d], arrived.at[row], s1.at[d], r1.at[d], (to, col)))
     fold(ops, h, f, hx, ht, folded, yb, ya)
+    pack(ya, wzo, wzb, wza, wys, wxo, wxs, wx0)
+    choose(neighbours, col, sel)
+    pl.semaphore_wait(barrier, len(peers))
+
+    arrivals = [
+        start_copy(leaving.at[d], arrived.at[row], s1.at[d], r1.at[d], ((row + d) % ROWS, col))
+        for d in range(1, ROWS)
+    ]
     for copy in arrivals:
         copy.wait_recv()
 
-    def place(at, carry):
-        wanted = at.astype(f32)
-        total = [jnp.zeros((8, 128), f32)] * 4
+    def place(group, carry):
+        total = [[jnp.zeros((8, 128), f32)] * 4 for n in range(4)]
         for k in range(ROWS):
             for s in range(2):
-                hit = jnp.broadcast_to(arrived[k, 64 + s : 65 + s, :], (8, 128)) == wanted
-                for c in range(4):
-                    start = s * 32 + c * 8
-                    total[c] = jnp.where(hit, arrived[k, start : start + 8, :], total[c])
-        for c in range(4):
-            boxes[0, at, c * 8 : (c + 1) * 8, :] = total[c]
-        return carry
-
-    lax.fori_loop(0, 16, place, 0)
-
-    hops = [
-        start_copy(boxes.at[0], boxes.at[1], s2.at[0], r2.at[0], ((row + 1) % ROWS, col)),
-        start_copy(boxes.at[0], boxes.at[2], s2.at[1], r2.at[1], ((row + ROWS - 1) % ROWS, col)),
-    ]
-    pack(ya, wzo, wzb, wza, wys, wxo, wxs, wx0)
-    choose(neighbours, col, sel)
+                tag = jnp.broadcast_to(arrived[k, 64 + s : 65 + s, :], (8, 128))
+                data = [arrived[k, s * 32 + c * 8 : s * 32 + c * 8 + 8, :] for c in range(4)]
+                for n in range(4):
+                    hit = tag == (group * 4 + n).astype(f32)
+                    total[n] = [jnp.where(hit, data[c], total[n][c]) for c in range(4)]
+        for n in range(4):
+            for c in range(4):
+                boxes[0, group * 4 + n, c * 8 : (c + 1) * 8, :] = total[n][c]
+        return carry
+
+    hops = []
+    for p in range(2):
+        lax.fori_loop(2 * p, 2 * p + 2, place, 0)
+        for k, to in ((1, (row + 1) % ROWS), (2, (row + ROWS - 1) % ROWS)):
+            at, n = pl.ds(8 * p, 8), 2 * p + k - 1
+            hops.append(start_copy(boxes.at[0, at], boxes.at[k, at], s2.at[n], r2.at[n], (to, col)))
     lay_out(boxes.at[0], lines, xs.at[0])
-    for hop, k in zip(hops, (1, 2)):
-        hop.wait_recv()
+    for k in (1, 2):
+        hops[k - 1].wait_recv()
+        hops[k + 1].wait_recv()
         lay_out(boxes.at[k], lines, xs.at[k])
 
     sides_lines(xs.at[1], xs.at[2], wzb, wza, wys, t_hi, t_lo, ya, yb, yc)
@@ -396,22 +397,27 @@
 
     def give_back(d, carry):
         to = (row + d) % ROWS
+        hit = []
         for s in range(2):
-            place = jnp.broadcast_to(arrived[to, pl.ds(64 + s, 1), :], (8, 128))
-            hit = [place == float(k) for k in range(16)]
-            for c in range(4):
-                rows = slice(c * 8, (c + 1) * 8)
-                v = result[0, rows, :]
-                for k in range(1, 16):
-                    v = jnp.where(hit[k], result[k, rows, :], v)
-                returned[d * 2 + s, rows, :] = v
-        return carry
-
-    lax.fori_loop(0, ROWS, give_back, 0)
+            tag = jnp.broadcast_to(arrived[to, 64 + s : 65 + s, :], (8, 128))
+            hit.append([tag == float(k) for k in range(16)])
+        for c in range(4):
+            rows = slice(c * 8, (c + 1) * 8)
+            v = [result[0, rows, :]] * 2
+            for k in range(1, 16):
+                box = result[k, rows, :]
+                v = [jnp.where(hit[s][k], box, v[s]) for s in range(2)]
+            for s in range(2):
+                returned[d * 2 + s, rows, :] = v[s]
+        return carry
+
     returns = []
-    for d in range(1, ROWS):
-        src, dst = returned.at[pl.ds(2 * d, 2)], back.at[pl.ds(row * 2, 2)]
-        returns.append(start_copy(src, dst, s6.at[d], r6.at[d], ((row + d) % ROWS, col)))
+    for first in range(1, ROWS, 3):
+        lax.fori_loop(first, first + 3, give_back, 0)
+        for d in range(first, first + 3):
+            src, dst = returned.at[pl.ds(2 * d, 2)], back.at[pl.ds(row * 2, 2)]
+            returns.append(start_copy(src, dst, s6.at[d], r6.at[d], ((row + d) % ROWS, col)))
+    give_back(0, 0)
     for s in range(2):
         back[row * 2 + s] = returned[s]
     for copy in returns:
@@ -441,7 +447,7 @@
             (4, 128, 128), (32, 32, 128), (32, 32, 128),
         )
     ]
-    scratch += [pltpu.SemaphoreType.DMA((n,)) for n in (16, 16, 2, 2, 4, 4, 12, 12, 16, 16)]
+    scratch += [pltpu.SemaphoreType.DMA((n,)) for n in (16, 16, 4, 4, 4, 4, 12, 12, 16, 16)]
     return pl.pallas_call(
         convolve_kernel,
         out_shape=jax.ShapeDtypeStruct((512, 128), f32),

time: 78 us -> 79.3 us (1.017)
  Pallas kernels: 75.1 us -> 76.5 us
    pallas_call x1, Pallas kernels: 75.1 us -> 76.5 us  [convolve(): pl.pallas_call(convolve_kernel, out_shape=jax.ShapeDtypeStruct((512, 128)...]
where the time goes in v4:
time: 79.3 us; the launch traced here: 78.1 us
  Pallas kernels  76.5 us (96%)
  local copies, waits for them, and re-layouts  1.67 us (2%)
    pallas_call x1, Pallas kernels, convolve(): pl.pallas_call(convolve_kernel, out_shape=jax.ShapeDtypeStruct((512, 128)...  76.5 us
    unnamed x1, local copies, waits for them, and re-layouts  1.67 us

profile of v4, /device:TPU:0, one launch (start us, length us, event | category | flops | bytes accessed | tf_op | source)
XLA Modules:
  0.0 78.1 jit_solution(1492576661885580761)
XLA Ops:
  0.0 76.5 %shard_map.55 = f32[512,128]{1,0:T(8,128)} custom-call(f32[512,128]{1,0:T(8,128)} %bitcast.14, s32[16]{0:T(128)} %slot.1, s32[6,16]{1,0:T(8,128)} %bitcast.15, f32[3,3,20,1024]{3,2,1,0:T(8,128)} %bitcast.13, f32[32,32]{1,0:T(8,128)} %h.1), custom_call_target="tpu_custom_call" | custom-call | tf_op jit(solution)/shard_map/pallas_call | solution.py:451
  76.5 1.7 %copy.7 = f32[16,4096]{1,0:T(8,128)} copy(f32[16,4096]{1,0:T(8,128)} %bitcast.12) | data formatting | bytes 524288

commit v5 on v4

--- a/solution.py
+++ b/solution.py
@@ -27,7 +27,7 @@
     return lax.broadcasted_iota(jnp.int32, (rows, 128), 1) < 64
 
 
-def centre_pass(xk, wz, wy, wx, t_hi, t_lo, ys, out):
+def centre_lines(xk, wz, wy, t_hi, t_lo, ys):
     mask = low_half(N)
 
     def pair(mp, carry):
@@ -48,6 +48,8 @@
 
     lax.fori_loop(0, PAIRS, pair, 0)
 
+
+def centre_columns(wx, ys, out):
     def column(b, carry):
         at = pl.ds(pl.multiple_of(b * OWN_LINE, 8), PAIRS * N)
         hi, lo = split(ys[at, :])
@@ -283,7 +285,7 @@
 
 def convolve_kernel(fine, slot, neighbours, ops, h, out, own, f, hx, ht,
                     wzo, wzb, wza, wys, wxo, wxs, wx0, sel, folded, leaving, arrived, boxes, lines, xs,
-                    t_hi, t_lo, ya, yb, yc, terms, part, centre, from_core, pair_sum, from_y, total,
+                    t_hi, t_lo, ya, yb, yc, terms, part, centre, from_core, pair_sum, from_y, relay, passing, total,
                     returned, back, s1, r1, s2, r2, s3, r3, s4, r4, s6, r6):
     row, col = lax.axis_index("row"), lax.axis_index("col")
     y, core = col // CORES, col % CORES
@@ -299,7 +301,13 @@
     slots = [slot[q] for q in range(16)]
     dest = [v // 128 for v in slots]
     first_row = lax.broadcasted_iota(jnp.int32, (8, 128), 0) == 0
-    for d in range(ROWS):
+    fold(ops, h, f, hx, ht, folded, yb, ya)
+    pack(ya, wzo, wzb, wza, wys, wxo, wxs, wx0)
+    choose(neighbours, col, sel)
+    pl.semaphore_wait(barrier, len(peers))
+
+    arrivals = []
+    for d in list(range(1, ROWS)) + [0]:
         to = (row + d) % ROWS
         target = arrived.at[row] if d == 0 else leaving.at[d]
         first, last = jnp.int32(16), jnp.int32(-1)
@@ -312,15 +320,8 @@
             target[k * N : (k + 1) * N, :] = own[q]
             tag.append(jnp.where(last >= 0, slot[q] % 16, -1).astype(f32))
         target[64:72, :] = jnp.where(first_row, tag[0], tag[1])
-    fold(ops, h, f, hx, ht, folded, yb, ya)
-    pack(ya, wzo, wzb, wza, wys, wxo, wxs, wx0)
-    choose(neighbours, col, sel)
-    pl.semaphore_wait(barrier, len(peers))
-
-    arrivals = [
-        start_copy(leaving.at[d], arrived.at[row], s1.at[d], r1.at[d], ((row + d) % ROWS, col))
-        for d in range(1, ROWS)
-    ]
+        if d:
+            arrivals.append(start_copy(leaving.at[d], arrived.at[row], s1.at[d], r1.at[d], (to, col)))
     for copy in arrivals:
         copy.wait_recv()
 
@@ -351,7 +352,7 @@
         lay_out(boxes.at[k], lines, xs.at[k])
 
     sides_lines(xs.at[1], xs.at[2], wzb, wza, wys, t_hi, t_lo, ya, yb, yc)
-    pairs, sums = [], []
+    pairs, sums = [], {}
     mask = low_half(128)
 
     def over_pair(c):
@@ -365,10 +366,22 @@
             v = jnp.where(mask, low, high)
             if d < Y - 1:
                 pair_sum[c, d] = v
-                k = c * (Y - 1) + d
-                sums.append(start_copy(pair_sum.at[c, d], from_y.at[c, d], s4.at[k], r4.at[k], across[d]))
             else:
                 total[c] = v
+        up, down, halves = across[0], across[2], (slice(0, 64), slice(64, 128))
+        for k, (d, half, to) in enumerate(((1, 0, up), (1, 1, down), (0, 1, up), (2, 0, down))):
+            src = pair_sum.at[c, d, halves[half]]
+            dst = relay.at[c, half] if d == 1 else from_y.at[c, d // 2, halves[half]]
+            sums[c, k] = start_copy(src, dst, s4.at[c * 6 + k], r4.at[c * 6 + k], to)
+
+    def relayed(c):
+        up, down, halves = across[0], across[2], (slice(0, 64), slice(64, 128))
+        for half, d, to in ((0, 0, up), (1, 2, down)):
+            sums[c, half].wait_recv()
+            passing[c, half] = pair_sum[c, d, halves[half]] + relay[c, half]
+            k = c * 6 + 4 + half
+            dst = from_y.at[c, d // 2, halves[half]]
+            sums[c, 4 + half] = start_copy(passing.at[c, half], dst, s4.at[k], r4.at[k], to)
 
     for c in range(4):
         sides_columns(8 * c, wxs, wx0, ya, yb, yc, terms)
@@ -377,14 +390,19 @@
         for k in range(Y):
             part[c, k // 2, k % 2] = summed[:, k * 128 : (k + 1) * 128]
         pairs.append(start_copy(part.at[c, 1 - core], from_core.at[c], s3.at[c], r3.at[c], sibling))
+        if c > 1:
+            relayed(c - 2)
         if c:
             over_pair(c - 1)
     over_pair(3)
-    centre_pass(xs.at[0], wzo, wys, wxo, t_hi, t_lo, ya, centre)
+    relayed(2)
+    centre_lines(xs.at[0], wzo, wys, t_hi, t_lo, ya)
+    relayed(3)
+    centre_columns(wxo, ya, centre)
     for c in range(4):
-        for d in range(Y - 1):
-            sums[c * (Y - 1) + d].wait_recv()
-        v = total[c] + from_y[c, 0] + from_y[c, 1] + from_y[c, 2]
+        for k in range(2, 6):
+            sums[c, k].wait_recv()
+        v = total[c] + from_y[c, 0] + from_y[c, 1]
         at = slice(c * 256, c * 256 + 128)
         centre[at, :] = centre[at, :] + v
         at = slice(c * 256 + 128, c * 256 + 256)
@@ -411,13 +429,11 @@
                 returned[d * 2 + s, rows, :] = v[s]
         return carry
 
+    lax.fori_loop(0, ROWS, give_back, 0)
     returns = []
-    for first in range(1, ROWS, 3):
-        lax.fori_loop(first, first + 3, give_back, 0)
-        for d in range(first, first + 3):
-            src, dst = returned.at[pl.ds(2 * d, 2)], back.at[pl.ds(row * 2, 2)]
-            returns.append(start_copy(src, dst, s6.at[d], r6.at[d], ((row + d) % ROWS, col)))
-    give_back(0, 0)
+    for d in range(1, ROWS):
+        src, dst = returned.at[pl.ds(2 * d, 2)], back.at[pl.ds(row * 2, 2)]
+        returns.append(start_copy(src, dst, s6.at[d], r6.at[d], ((row + d) % ROWS, col)))
     for s in range(2):
         back[row * 2 + s] = returned[s]
     for copy in returns:
@@ -427,7 +443,7 @@
         for k in range(q):
             earlier = jnp.where(dest[k] == dest[q], 1, earlier)
         out[pl.ds(q // 8 * 256 + q % 8, N, stride=8), :] = back[2 * dest[q] + earlier]
-    for copy in arrivals + pairs + sums + returns:
+    for copy in arrivals + pairs + list(sums.values()) + returns:
         copy.wait_send()
 
 
@@ -443,11 +459,11 @@
     scratch += [
         pltpu.VMEM(shape, f32)
         for shape in (
-            (256, 384), (4, 2, 2, 256, 128), (1024, 128), (4, 2, 256, 128), (4, 3, 128, 128), (4, 3, 128, 128),
-            (4, 128, 128), (32, 32, 128), (32, 32, 128),
+            (256, 384), (4, 2, 2, 256, 128), (1024, 128), (4, 2, 256, 128), (4, 3, 128, 128), (4, 2, 128, 128),
+            (4, 2, 64, 128), (4, 2, 64, 128), (4, 128, 128), (32, 32, 128), (32, 32, 128),
         )
     ]
-    scratch += [pltpu.SemaphoreType.DMA((n,)) for n in (16, 16, 4, 4, 4, 4, 12, 12, 16, 16)]
+    scratch += [pltpu.SemaphoreType.DMA((n,)) for n in (16, 16, 4, 4, 4, 4, 24, 24, 16, 16)]
     return pl.pallas_call(
         convolve_kernel,
         out_shape=jax.ShapeDtypeStruct((512, 128), f32),

time: 79.3 us -> 82.5 us (1.040)
  Pallas kernels: 76.5 us -> 80.4 us
    pallas_call x1, Pallas kernels: 76.5 us -> 80.4 us  [convolve(): pl.pallas_call(convolve_kernel, out_shape=jax.ShapeDtypeStruct((512, 128)...]
where the time goes in v5:
time: 82.5 us; the launch traced here: 82.1 us
  Pallas kernels  80.4 us (97%)
  local copies, waits for them, and re-layouts  1.67 us (2%)
    pallas_call x1, Pallas kernels, convolve(): pl.pallas_call(convolve_kernel, out_shape=jax.ShapeDtypeStruct((512, 128)...  80.4 us
    unnamed x1, local copies, waits for them, and re-layouts  1.67 us

profile of v5, /device:TPU:0, one launch (start us, length us, event | category | flops | bytes accessed | tf_op | source)
XLA Modules:
  0.0 82.1 jit_solution(17667115902435417463)
XLA Ops:
  0.0 80.4 %shard_map.55 = f32[512,128]{1,0:T(8,128)} custom-call(f32[512,128]{1,0:T(8,128)} %bitcast.14, s32[16]{0:T(128)} %slot.1, s32[6,16]{1,0:T(8,128)} %bitcast.15, f32[3,3,20,1024]{3,2,1,0:T(8,128)} %bitcast.13, f32[32,32]{1,0:T(8,128)} %h.1), custom_call_target="tpu_custom_call" | custom-call | tf_op jit(solution)/shard_map/pallas_call | solution.py:467
  80.4 1.7 %copy.7 = f32[16,4096]{1,0:T(8,128)} copy(f32[16,4096]{1,0:T(8,128)} %bitcast.12) | data formatting | bytes 524288

commit v6 on v4

--- a/solution.py
+++ b/solution.py
@@ -27,7 +27,7 @@
     return lax.broadcasted_iota(jnp.int32, (rows, 128), 1) < 64
 
 
-def centre_pass(xk, wz, wy, wx, t_hi, t_lo, ys, out):
+def centre_lines(xk, wz, wy, t_hi, t_lo, ys):
     mask = low_half(N)
 
     def pair(mp, carry):
@@ -48,6 +48,8 @@
 
     lax.fori_loop(0, PAIRS, pair, 0)
 
+
+def centre_columns(wx, ys, out):
     def column(b, carry):
         at = pl.ds(pl.multiple_of(b * OWN_LINE, 8), PAIRS * N)
         hi, lo = split(ys[at, :])
@@ -299,7 +301,10 @@
     slots = [slot[q] for q in range(16)]
     dest = [v // 128 for v in slots]
     first_row = lax.broadcasted_iota(jnp.int32, (8, 128), 0) == 0
-    for d in range(ROWS):
+    pl.semaphore_wait(barrier, len(peers))
+
+    arrivals = []
+    for d in list(range(1, ROWS)) + [0]:
         to = (row + d) % ROWS
         target = arrived.at[row] if d == 0 else leaving.at[d]
         first, last = jnp.int32(16), jnp.int32(-1)
@@ -312,15 +317,11 @@
             target[k * N : (k + 1) * N, :] = own[q]
             tag.append(jnp.where(last >= 0, slot[q] % 16, -1).astype(f32))
         target[64:72, :] = jnp.where(first_row, tag[0], tag[1])
+        if d:
+            arrivals.append(start_copy(leaving.at[d], arrived.at[row], s1.at[d], r1.at[d], (to, col)))
     fold(ops, h, f, hx, ht, folded, yb, ya)
     pack(ya, wzo, wzb, wza, wys, wxo, wxs, wx0)
     choose(neighbours, col, sel)
-    pl.semaphore_wait(barrier, len(peers))
-
-    arrivals = [
-        start_copy(leaving.at[d], arrived.at[row], s1.at[d], r1.at[d], ((row + d) % ROWS, col))
-        for d in range(1, ROWS)
-    ]
     for copy in arrivals:
         copy.wait_recv()
 
@@ -380,7 +381,8 @@
         if c:
             over_pair(c - 1)
     over_pair(3)
-    centre_pass(xs.at[0], wzo, wys, wxo, t_hi, t_lo, ya, centre)
+    centre_lines(xs.at[0], wzo, wys, t_hi, t_lo, ya)
+    centre_columns(wxo, ya, centre)
     for c in range(4):
         for d in range(Y - 1):
             sums[c * (Y - 1) + d].wait_recv()
@@ -411,13 +413,11 @@
                 returned[d * 2 + s, rows, :] = v[s]
         return carry
 
+    lax.fori_loop(0, ROWS, give_back, 0)
     returns = []
-    for first in range(1, ROWS, 3):
-        lax.fori_loop(first, first + 3, give_back, 0)
-        for d in range(first, first + 3):
-            src, dst = returned.at[pl.ds(2 * d, 2)], back.at[pl.ds(row * 2, 2)]
-            returns.append(start_copy(src, dst, s6.at[d], r6.at[d], ((row + d) % ROWS, col)))
-    give_back(0, 0)
+    for d in range(1, ROWS):
+        src, dst = returned.at[pl.ds(2 * d, 2)], back.at[pl.ds(row * 2, 2)]
+        returns.append(start_copy(src, dst, s6.at[d], r6.at[d], ((row + d) % ROWS, col)))
     for s in range(2):
         back[row * 2 + s] = returned[s]
     for copy in returns:

time: 79.3 us -> 76.3 us (0.962)
  Pallas kernels: 76.5 us -> 73.5 us
    pallas_call x1, Pallas kernels: 76.5 us -> 73.5 us  [convolve(): pl.pallas_call(convolve_kernel, out_shape=jax.ShapeDtypeStruct((512, 128)...]
where the time goes in v6:
time: 76.3 us; the launch traced here: 75.2 us
  Pallas kernels  73.5 us (96%)
  local copies, waits for them, and re-layouts  1.67 us (2%)
    pallas_call x1, Pallas kernels, convolve(): pl.pallas_call(convolve_kernel, out_shape=jax.ShapeDtypeStruct((512, 128)...  73.5 us
    unnamed x1, local copies, waits for them, and re-layouts  1.67 us

profile of v6, /device:TPU:0, one launch (start us, length us, event | category | flops | bytes accessed | tf_op | source)
XLA Modules:
  0.0 75.2 jit_solution(8352739930355967382)
XLA Ops:
  0.0 73.5 %shard_map.55 = f32[512,128]{1,0:T(8,128)} custom-call(f32[512,128]{1,0:T(8,128)} %bitcast.14, s32[16]{0:T(128)} %slot.1, s32[6,16]{1,0:T(8,128)} %bitcast.15, f32[3,3,20,1024]{3,2,1,0:T(8,128)} %bitcast.13, f32[32,32]{1,0:T(8,128)} %h.1), custom_call_target="tpu_custom_call" | custom-call | tf_op jit(solution)/shard_map/pallas_call | solution.py:451
  73.5 1.7 %copy.7 = f32[16,4096]{1,0:T(8,128)} copy(f32[16,4096]{1,0:T(8,128)} %bitcast.12) | data formatting | bytes 524288

commit v7 on v6

--- a/solution.py
+++ b/solution.py
@@ -32,11 +32,11 @@
 
     def pair(mp, carry):
         weights = wz[pl.ds(pl.multiple_of(mp * 128, 128), 128), 0:192]
-        for q in range(4):
-            z = dot_t(xk[q * 256 : (q + 1) * 256, 0:192], weights)
+        for q in range(1):
+            z = dot_t(xk[q * 1024 : (q + 1) * 1024, 0:192], weights)
             hi, lo = split(z)
-            t_hi[q * 256 : (q + 1) * 256, 0:128] = hi
-            t_lo[q * 256 : (q + 1) * 256, 0:128] = lo
+            t_hi[q * 1024 : (q + 1) * 1024, 0:128] = hi
+            t_lo[q * 1024 : (q + 1) * 1024, 0:128] = lo
         left = jnp.concatenate([wy[mp * 2, 0:N, 0:96], wy[mp * 2 + 1, 0:N, 0:96]], axis=0)
 
         for i in range(N):
@@ -58,7 +58,7 @@
         out[pl.ds(pl.multiple_of(b * N, N), N), :] = r[:N] + pltpu.roll(r[N:], 64, 1)
         return carry
 
-    lax.fori_loop(0, N, column, 0, unroll=4)
+    lax.fori_loop(0, N, column, 0, unroll=8)
 
 
 def sides_lines(xkb, xka, wzb, wza, wy, t_hi, t_lo, ya, yb, yc):
@@ -67,14 +67,14 @@
     def pair(mp, carry):
         for xk, wz, base in ((xkb, wzb, 0), (xka, wza, 128)):
             weights = wz[pl.ds(pl.multiple_of(mp * 256, 256), 256), 0:192]
-            for q in range(4):
-                z = dot_t(xk[q * 256 : (q + 1) * 256, 0:192], weights)
+            for q in range(1):
+                z = dot_t(xk[q * 1024 : (q + 1) * 1024, 0:192], weights)
                 hi, lo = split(z)
                 for odd in range(2):
-                    t_hi[odd * 1024 + q * 256 : odd * 1024 + (q + 1) * 256, base : base + 128] = hi[
+                    t_hi[odd * 1024 + q * 1024 : odd * 1024 + (q + 1) * 1024, base : base + 128] = hi[
                         :, odd * 128 : (odd + 1) * 128
                     ]
-                    t_lo[odd * 1024 + q * 256 : odd * 1024 + (q + 1) * 256, base : base + 128] = lo[
+                    t_lo[odd * 1024 + q * 1024 : odd * 1024 + (q + 1) * 1024, base : base + 128] = lo[
                         :, odd * 128 : (odd + 1) * 128
                     ]
         for odd in range(2):
@@ -113,7 +113,7 @@
         out[rows, 256:384] = first[:N] + first[N:] + dot(wx0[0:N, :], lo)
         return carry
 
-    lax.fori_loop(0, 8, column, 0, unroll=4)
+    lax.fori_loop(0, 8, column, 0, unroll=8)
 
 
 def spread(h, lanes, pick):
@@ -357,7 +357,7 @@
 
     def over_pair(c):
         pairs[c].wait_recv()
-        for d in range(Y):
+        for d in (1, 0, 2, 3):
             to = (y + 1 + d) % Y
             v = part[c, core, to // 2] + from_core[c, to // 2]
             odd = to % 2 == 1

time: 76.3 us -> 74.7 us (0.979)
  Pallas kernels: 73.5 us -> 71.9 us
    pallas_call x1, Pallas kernels: 73.5 us -> 71.9 us  [convolve(): pl.pallas_call(convolve_kernel, out_shape=jax.ShapeDtypeStruct((512, 128)...]
where the time goes in v7:
time: 74.7 us; the launch traced here: 73.5 us
  Pallas kernels  71.9 us (96%)
  local copies, waits for them, and re-layouts  1.67 us (2%)
    pallas_call x1, Pallas kernels, convolve(): pl.pallas_call(convolve_kernel, out_shape=jax.ShapeDtypeStruct((512, 128)...  71.9 us
    unnamed x1, local copies, waits for them, and re-layouts  1.67 us

profile of v7, /device:TPU:0, one launch (start us, length us, event | category | flops | bytes accessed | tf_op | source)
XLA Modules:
  0.0 73.5 jit_solution(2180997161313395813)
XLA Ops:
  0.0 71.9 %shard_map.55 = f32[512,128]{1,0:T(8,128)} custom-call(f32[512,128]{1,0:T(8,128)} %bitcast.14, s32[16]{0:T(128)} %slot.1, s32[6,16]{1,0:T(8,128)} %bitcast.15, f32[3,3,20,1024]{3,2,1,0:T(8,128)} %bitcast.13, f32[32,32]{1,0:T(8,128)} %h.1), custom_call_target="tpu_custom_call" | custom-call | tf_op jit(solution)/shard_map/pallas_call | solution.py:451
  71.9 1.7 %copy.7 = f32[16,4096]{1,0:T(8,128)} copy(f32[16,4096]{1,0:T(8,128)} %bitcast.12) | data formatting | bytes 524288

commit v8 on v7

--- a/solution.py
+++ b/solution.py
@@ -206,6 +206,7 @@
 
 MESH = pl.DeviceIdType.MESH
 Y, CORES, ROWS = 4, 2, 16
+FAR_FIRST = (10, 6, 9, 11, 14, 2, 8, 5, 7, 13, 15, 1, 3, 4, 12)
 
 
 def start_copy(src, dst, s, r, peer):
@@ -304,7 +305,7 @@
     pl.semaphore_wait(barrier, len(peers))
 
     arrivals = []
-    for d in list(range(1, ROWS)) + [0]:
+    for d in FAR_FIRST + (0,):
         to = (row + d) % ROWS
         target = arrived.at[row] if d == 0 else leaving.at[d]
         first, last = jnp.int32(16), jnp.int32(-1)
@@ -415,7 +416,7 @@
 
     lax.fori_loop(0, ROWS, give_back, 0)
     returns = []
-    for d in range(1, ROWS):
+    for d in FAR_FIRST:
         src, dst = returned.at[pl.ds(2 * d, 2)], back.at[pl.ds(row * 2, 2)]
         returns.append(start_copy(src, dst, s6.at[d], r6.at[d], ((row + d) % ROWS, col)))
     for s in range(2):

time: 74.7 us -> 75.3 us (level)
  no operation moved by 1% of the time
where the time goes in v8:
time: 75.3 us; the launch traced here: 74.2 us
  Pallas kernels  72.5 us (96%)
  local copies, waits for them, and re-layouts  1.67 us (2%)
    pallas_call x1, Pallas kernels, convolve(): pl.pallas_call(convolve_kernel, out_shape=jax.ShapeDtypeStruct((512, 128)...  72.5 us
    unnamed x1, local copies, waits for them, and re-layouts  1.67 us

profile of v8, /device:TPU:0, one launch (start us, length us, event | category | flops | bytes accessed | tf_op | source)
XLA Modules:
  0.0 74.2 jit_solution(8674561853495461151)
XLA Ops:
  0.0 72.5 %shard_map.55 = f32[512,128]{1,0:T(8,128)} custom-call(f32[512,128]{1,0:T(8,128)} %bitcast.14, s32[16]{0:T(128)} %slot.1, s32[6,16]{1,0:T(8,128)} %bitcast.15, f32[3,3,20,1024]{3,2,1,0:T(8,128)} %bitcast.13, f32[32,32]{1,0:T(8,128)} %h.1), custom_call_target="tpu_custom_call" | custom-call | tf_op jit(solution)/shard_map/pallas_call | solution.py:452
  72.5 1.7 %copy.7 = f32[16,4096]{1,0:T(8,128)} copy(f32[16,4096]{1,0:T(8,128)} %bitcast.12) | data formatting | bytes 524288
